TPU v7x, 128 devices: a whole 4x4x4 slice. The times are simulated.
128 devices in a mesh: row: 32 (over y, x, core), col: 4 (over z).
Axes of the slice: x: 4, y: 4, z: 4, core: 2. Of those that a mesh axis runs over, the one named last changes fastest.
Arguments:
- layer_input: bfloat16 [1024, 6144], P('row', 'col'), may hold values from -6 to 6
- out_cotangent: bfloat16 [1024, 6144], P('row', 'col'), may hold values from -6 to 6
- preact: bfloat16 [1024, 49152], P('col', 'row'), may hold values from -8 to 8
- up_weight: bfloat16 [6144, 49152], P('col', 'row'), may hold values from -0.078125 to 0.078125
- down_weight: bfloat16 [49152, 6144], P('row', 'col'), may hold values from -0.02734375 to 0.02734375
Outputs:
- input_grad: bfloat16 [1024, 6144], P('row', 'col')
- up_grad: bfloat16 [6144, 49152], P('col', 'row')
- down_grad: bfloat16 [49152, 6144], P('row', 'col')
All inputs are finite; a program needn't handle non-finite values.
Results may differ from a plain program's by a relative error of at most 0.02.
Values may be sent and summed in bfloat16 or wider, within the bound.
No kernel may reach another device: no remote copies, remote signals or barrier semaphores. Data moves between devices by JAX's collectives and lax.ppermute only.
A program may use at most 128 MiB of HBM per device.

v0:
```python
import math

import jax
import jax.numpy as jnp
from jax import lax
from jax.sharding import PartitionSpec as P


def gelu_parts(pre):
    coeff = math.sqrt(2.0 / math.pi)
    inner = coeff * (pre + 0.044715 * pre * pre * pre)
    tangent = jnp.tanh(inner)
    activated = 0.5 * pre * (1.0 + tangent)
    slope = 0.5 * (1.0 + tangent) + 0.5 * pre * (1.0 - tangent * tangent) * coeff * (
        1.0 + 3.0 * 0.044715 * pre * pre
    )
    return (activated, slope)


def local(layer_input, out_cotangent, preact, up_weight, down_weight):
    input_all, cotangent_all = (
        lax.all_gather(layer_input, "row", axis=0, tiled=True),
        lax.all_gather(out_cotangent, "row", axis=0, tiled=True),
    )
    activated_f32, slope = gelu_parts(preact.astype(jnp.float32))
    activated = activated_f32.astype(jnp.bfloat16)
    act_grad = lax.psum_scatter(
        lax.dot_general(
            cotangent_all, down_weight, (((1,), (1,)), ((), ())), preferred_element_type=jnp.float32
        ),
        "col",
        scatter_dimension=0,
        tiled=True,
    )
    hidden_grad = (act_grad * slope).astype(jnp.bfloat16)
    activated_all, hidden_all = (
        lax.all_gather(activated, "col", axis=0, tiled=True),
        lax.all_gather(hidden_grad, "col", axis=0, tiled=True),
    )
    down_grad = lax.dot_general(
        activated_all, cotangent_all, (((0,), (0,)), ((), ())), preferred_element_type=jnp.float32
    ).astype(jnp.bfloat16)
    up_sum = lax.dot_general(
        input_all, hidden_all, (((0,), (0,)), ((), ())), preferred_element_type=jnp.float32
    )
    up_grad = up_sum.astype(jnp.bfloat16)
    input_grad = lax.psum_scatter(
        lax.dot_general(
            hidden_all, up_weight, (((1,), (1,)), ((), ())), preferred_element_type=jnp.float32
        ).astype(jnp.bfloat16),
        "row",
        scatter_dimension=0,
        tiled=True,
    )
    return (input_grad, up_grad, down_grad)


def solution(mesh):
    in_specs = (P("row", "col"), P("row", "col"), P("col", "row"), P("col", "row"), P("row", "col"))
    out_specs = (P("row", "col"), P("col", "row"), P("row", "col"))
    return jax.shard_map(local, mesh=mesh, in_specs=in_specs, out_specs=out_specs, check_vma=False)
```

profile of v0, /device:TPU:1, one launch (start us, length us, event | category | flops | bytes accessed | tf_op | source)
XLA Modules:
  0.0 352.6 jit_solution(8288338917896607214)
XLA Ops:
  7.2 0.0 all-gather.5.cloned.1.call-start
  7.2 0.7 all-gather.5.cloned.1.call-update
  7.9 0.0 reduce-scatter.3.cloned.1.call-start
  7.9 50.9 %all-gather.5.cloned.1.call-done = bf16[1024,1536]{1,0:T(8,128)(2,1)} async-done(((bf16[32,1536]{1,0:T(8,128)(2,1)}), bf16[1024,1536]{1,0:T(8,128)(2,1)}) %all-gather.5.cloned.1.call-update) | async-done | bytes 3145744 | tf_op jit(solution)/shard_map/all_gather | solution.py:23
  58.8 9.8 %fusion.12 = f32[1024,1536]{1,0:T(8,128)} fusion(bf16[1024,1536]{1,0:T(8,128)(2,1)} %all-gather.5.cloned.1.call-done, bf16[1536,1536]{1,0:T(8,128)(2,1)} %param.9), kind=kOutput, calls=%fused_computation.22 | convolution fusion | flops 4831838208 | bytes 14155776 | tf_op jit(solution)/shard_map/dot_general | solution.py:28
  68.6 0.0 copy-start
  68.6 0.0 reduce-scatter.3.cloned.1.call-update
  68.7 0.0 all-gather.7.cloned.1.call-start
  68.7 63.3 %reduce-scatter.3.cloned.1.call-done = f32[256,1536]{1,0:T(8,128)} async-done(((f32[1024,1536]{1,0:T(8,128)}), f32[256,1536]{1,0:T(8,128)}) %reduce-scatter.3.cloned.1.call-update) | async-done | bytes 1572880 | tf_op jit(solution)/shard_map/reduce_scatter | solution.py:27
  132.0 0.0 copy-done
  132.0 3.7 %fusion.8 = (bf16[256,1536]{1,0:T(8,128)(2,1)}, bf16[256,1536]{1,0:T(8,128)(2,1)}) fusion(bf16[256,1536]{1,0:T(8,128)(2,1)S(1)} %copy-done, f32[256,1536]{1,0:T(8,128)} %reduce-scatter.3.cloned.1.call-done), kind=kLoop, calls=%fused_computation.18 | loop fusion | flops 8650752 | bytes 3932160 | tf_op jit(solution)/shard_map/convert_element_type | solution.py:26
  135.7 0.0 all-gather.7.cloned.1.call-update
  135.7 0.0 all-gather.9.cloned.1.call-start
  135.8 0.5 all-gather.9.cloned.1.call-update
  136.3 0.0 all-gather.11.cloned.1.call-start
  136.4 0.5 all-gather.11.cloned.1.call-update
  136.9 0.0 reduce-scatter.5.cloned.1.call-start
  137.0 38.2 %all-gather.7.cloned.1.call-done = bf16[1024,1536]{1,0:T(8,128)(2,1)} async-done(((bf16[256,1536]{1,0:T(8,128)(2,1)}), bf16[1024,1536]{1,0:T(8,128)(2,1)}) %all-gather.7.cloned.1.call-update) | async-done | bytes 3145744 | tf_op jit(solution)/shard_map/all_gather | solution.py:38
  175.2 9.3 %convolution_convert_fusion.2 = bf16[1024,1536]{1,0:T(8,128)(2,1)} fusion(bf16[1024,1536]{1,0:T(8,128)(2,1)} %all-gather.7.cloned.1.call-done, bf16[1536,1536]{1,0:T(8,128)(2,1)} %param.8), kind=kOutput, calls=%fused_computation.10 | convolution fusion | flops 4833411072 | bytes 11010048 | tf_op jit(solution)/shard_map/dot_general | solution.py:48
  184.5 0.0 copy-start.2
  184.5 0.0 reduce-scatter.5.cloned.1.call-update
  184.5 38.2 %all-gather.9.cloned.1.call-done = bf16[1024,1536]{1,0:T(8,128)(2,1)} async-done(((bf16[32,1536]{1,0:T(8,128)(2,1)}), bf16[1024,1536]{1,0:T(8,128)(2,1)}) %all-gather.9.cloned.1.call-update) | async-done | bytes 3145744 | tf_op jit(solution)/shard_map/all_gather | solution.py:22
  222.7 0.0 copy-done.2
  222.7 8.6 %fusion = bf16[1536,1536]{0,1:T(8,128)(2,1)} fusion(bf16[1024,1536]{1,0:T(8,128)(2,1)S(1)} %copy-done.2, bf16[1024,1536]{1,0:T(8,128)(2,1)} %all-gather.9.cloned.1.call-done), kind=kOutput, calls=%fused_computation.2 | convolution fusion | flops 4834197504 | bytes 11010048 | tf_op jit(solution)/shard_map/dot_general | solution.py:43
  231.3 0.0 copy-start.1
  231.3 7.0 %copy.8 = bf16[1536,1536]{1,0:T(8,128)(2,1)} copy(bf16[1536,1536]{0,1:T(8,128)(2,1)} %fusion) | data formatting | bytes 9437184
  238.3 24.7 %all-gather.11.cloned.1.call-done = bf16[1024,1536]{1,0:T(8,128)(2,1)} async-done(((bf16[256,1536]{1,0:T(8,128)(2,1)}), bf16[1024,1536]{1,0:T(8,128)(2,1)}) %all-gather.11.cloned.1.call-update) | async-done | bytes 3145744 | tf_op jit(solution)/shard_map/all_gather | solution.py:37
  263.0 0.0 copy-done.1
  263.0 8.7 %convolution_convert_fusion = bf16[1536,1536]{1,0:T(8,128)(2,1)} fusion(bf16[1024,1536]{1,0:T(8,128)(2,1)} %all-gather.11.cloned.1.call-done, bf16[1024,1536]{1,0:T(8,128)(2,1)S(1)} %copy-done.1), kind=kOutput, calls=%fused_computation | convolution fusion | flops 4834197504 | bytes 11010048 | tf_op jit(solution)/shard_map/dot_general | solution.py:40
  271.7 74.0 %reduce-scatter.5.cloned.1.call-done = bf16[32,1536]{1,0:T(8,128)(2,1)} async-done(((bf16[1024,1536]{1,0:T(8,128)(2,1)}), bf16[32,1536]{1,0:T(8,128)(2,1)}) %reduce-scatter.5.cloned.1.call-update) | async-done | bytes 98320 | tf_op jit(solution)/shard_map/reduce_scatter | solution.py:47
Async XLA Ops:
  7.2 51.7 %all-gather.5.cloned.1.call-start = ((), (), s32[]{:S(2)}) async-start(), calls=%async_computation.2 | async-start | bytes 3244032 | tf_op jit(solution)/shard_map/all_gather | solution.py:23
  7.9 124.1 %reduce-scatter.3.cloned.1.call-start = ((), (), s32[]{:S(2)}) async-start(), calls=%async_computation.3 | async-start | bytes 7864320 | tf_op jit(solution)/shard_map/reduce_scatter | solution.py:27
  68.6 63.4 %copy-start = (bf16[256,1536]{1,0:T(8,128)(2,1)S(1)}, bf16[256,1536]{1,0:T(8,128)(2,1)}, u32[]{:S(2)}) copy-start(bf16[256,1536]{1,0:T(8,128)(2,1)} %param.7) | copy-start | bytes 2359300
  68.7 106.5 %all-gather.7.cloned.1.call-start = ((), (), s32[]{:S(2)}) async-start(), calls=%async_computation.4 | async-start | bytes 3932160 | tf_op jit(solution)/shard_map/all_gather | solution.py:38
  135.7 86.9 %all-gather.9.cloned.1.call-start = ((), (), s32[]{:S(2)}) async-start(), calls=%async_computation.6 | async-start | bytes 3244032 | tf_op jit(solution)/shard_map/all_gather | solution.py:22
  136.3 126.7 %all-gather.11.cloned.1.call-start = ((), (), s32[]{:S(2)}) async-start(), calls=%async_computation.7 | async-start | bytes 3932160 | tf_op jit(solution)/shard_map/all_gather | solution.py:37
  136.9 208.8 %reduce-scatter.5.cloned.1.call-start = ((), (), s32[]{:S(2)}) async-start(), calls=%async_computation.5 | async-start | bytes 3244032 | tf_op jit(solution)/shard_map/reduce_scatter | solution.py:47
  184.5 38.2 %copy-start.2 = (bf16[1024,1536]{1,0:T(8,128)(2,1)S(1)}, bf16[1024,1536]{1,0:T(8,128)(2,1)}, u32[]{:S(2)}) copy-start(bf16[1024,1536]{1,0:T(8,128)(2,1)} %all-gather.7.cloned.1.call-done) | copy-start | bytes 9437188
  231.3 31.7 %copy-start.1 = (bf16[1024,1536]{1,0:T(8,128)(2,1)S(1)}, bf16[1024,1536]{1,0:T(8,128)(2,1)}, u32[]{:S(2)}) copy-start(bf16[1024,1536]{1,0:T(8,128)(2,1)} %all-gather.5.cloned.1.call-done) | copy-start | bytes 9437188
Sparse Core Ops, SparseCore 0:
  10.2 48.5 all-gather.4
  68.8 63.2 reduce-scatter.2
  135.9 39.2 all-gather.6
  177.3 45.3 all-gather.8
  224.2 38.7 all-gather.10
  267.1 78.6 reduce-scatter.4
where the time goes:
time: 354 us; the launch traced here: 353 us
  waiting for transfers between devices  291 us (82%)
  matrix products  36.4 us (10%)
  between operations  14.1 us (4%)
  local copies, waits for them, and re-layouts  7.04 us (2%)
  other arithmetic  3.67 us (1%)
    reduce_scatter x1, waiting for transfers between devices, local(): lax.psum_scatter(lax.dot_general(hidden_all, up_weight, (((1,), (1,)), ((...  74 us
    reduce_scatter x1, waiting for transfers between devices, local(): lax.psum_scatter(lax.dot_general(cotangent_all, down_weight, (((1,), (1,)...  63.3 us
    all_gather x1, waiting for transfers between devices, local(): lax.all_gather(out_cotangent, 'row', axis=0, tiled=True)  50.9 us
    all_gather x1, waiting for transfers between devices, local(): lax.all_gather(hidden_grad, 'col', axis=0, tiled=True)  38.2 us
    all_gather x1, waiting for transfers between devices, local(): lax.all_gather(layer_input, 'row', axis=0, tiled=True)  38.2 us
    all_gather x1, waiting for transfers between devices, local(): lax.all_gather(activated, 'col', axis=0, tiled=True)  24.7 us
    dot_general x1, matrix products, local(): lax.dot_general(cotangent_all, down_weight, (((1,), (1,)), ((), ())), pre...  9.78 us
    dot_general x1, matrix products, local(): lax.dot_general(hidden_all, up_weight, (((1,), (1,)), ((), ())), preferre...  9.29 us
  transfers between devices with their start and end apart: 6, of which 6 were waited for; matrix products, arithmetic and copies ran while one was open for 10% of the time, Pallas kernels for 0%

commit v1 on v0

v1 whole, which is shorter than its diff:
```python
import math

import jax
import jax.numpy as jnp
from jax import lax
from jax.sharding import PartitionSpec as P

BF16 = jnp.bfloat16
F32 = jnp.float32
NY, NX, NZ = 4, 4, 4
CHUNKS = 2
SHIFTS = (1, -1, 2)


def device(y, x, core):
    return ((y % NY) * NX + x % NX) * 2 + core


def places():
    return [(y, x, core) for y in range(NY) for x in range(NX) for core in range(2)]


SIBLING = [(device(y, x, c), device(y, x, 1 - c)) for y, x, c in places()]


def plane_step(shift, x_core):
    return [
        (device(y, x, c), device(y, x + shift, c) if c == x_core else device(y + shift, x, c))
        for y, x, c in places()
    ]


def z_step(shift):
    return [(z, (z + shift) % NZ) for z in range(NZ)]


Z_BY_CORE = [
    (device(y, x, c) * NZ + z, device(y, x, c) * NZ + (z + (1 if c == 0 else -1)) % NZ)
    for y, x, c in places()
    for z in range(NZ)
]


def swap_cores(v):
    return lax.ppermute(v, "row", SIBLING)


def send_z(v, shift):
    return lax.ppermute(v, "col", z_step(shift))


def send_z_by_core(v):
    return lax.ppermute(v, ("row", "col"), Z_BY_CORE)


def dot(a, b, ca, cb):
    return lax.dot_general(a, b, (((ca,), (cb,)), ((), ())), preferred_element_type=F32)


def put(buf, piece, index):
    start = (index % buf.shape[0],) + (0,) * (buf.ndim - 1)
    return lax.dynamic_update_slice(buf, piece[None], start)


def take(buf, index):
    return lax.dynamic_index_in_dim(buf, index % buf.shape[0], 0, keepdims=False)


def gelu_parts(pre):
    coeff = math.sqrt(2.0 / math.pi)
    tangent = jnp.tanh(coeff * (pre + 0.044715 * pre * pre * pre))
    activated = 0.5 * pre * (1.0 + tangent)
    slope = 0.5 * (1.0 + tangent) + 0.5 * pre * (1.0 - tangent * tangent) * coeff * (
        1.0 + 3.0 * 0.044715 * pre * pre
    )
    return (activated, slope)


def after(v, *done):
    return lax.optimization_barrier((v,) + done)[0]


def ordered(even, ours, other, axis):
    return jnp.where(
        even, jnp.concatenate([ours, other], axis), jnp.concatenate([other, ours], axis)
    )


def halves(v, even):
    n = v.shape[-1] // 2
    left, right = v[..., :n], v[..., n:]
    return jnp.where(even, left, right), jnp.where(even, right, left)


def line_send(v, x_core):
    return [lax.ppermute(v, "row", plane_step(shift, x_core)) for shift in SHIFTS]


def line_join(v, pieces, place):
    out = put(jnp.zeros((4,) + v.shape, v.dtype), v, place)
    for shift, piece in zip(SHIFTS, pieces):
        out = put(out, piece, place - shift)
    return out


def line_reduce(v, place, x_core):
    pieces = [
        lax.ppermute(take(v, place + shift), "row", plane_step(shift, x_core)) for shift in SHIFTS
    ]
    total = take(v, place).astype(F32)
    for piece in pieces:
        total = total + piece.astype(F32)
    return total


def local(layer_input, out_cotangent, preact, up_weight, down_weight):
    row, z = lax.axis_index("row"), lax.axis_index("col")
    even, x, y = row % 2 == 0, (row // 2) % NX, row // (2 * NX)
    first, second = jnp.where(even, x, y), jnp.where(even, y, x)

    ours, theirs = halves(jnp.stack([out_cotangent, layer_input]), even)
    pair = ordered(even, ours, swap_cores(theirs), 1)
    pieces = line_send(pair, 0)
    cot_line = line_join(pair[0], [p[0] for p in pieces], first)
    input_line = line_join(pair[1], [p[1] for p in pieces], first)

    activated, slope = gelu_parts(after(preact, pair).astype(F32))
    activated = activated.astype(BF16)
    act_below, act_above = send_z(activated, 1), send_z(activated, -1)

    pieces = line_send(cot_line, 1)
    cot = line_join(cot_line, pieces, second)
    cot = jnp.where(even, cot, cot.swapaxes(0, 1)).reshape(-1, cot.shape[-1])
    cot = ordered(even, cot, swap_cores(cot), 1)
    tokens = cot.reshape(NZ, -1, cot.shape[1])
    slope = after(slope, cot_line)

    pieces = line_send(after(input_line, cot), 1)
    inputs = line_join(input_line, pieces, second)
    inputs = jnp.where(even, inputs, inputs.swapaxes(0, 1)).reshape(-1, inputs.shape[-1])
    inputs = ordered(even, inputs, swap_cores(inputs), 1)

    width = down_weight.shape[0] // CHUNKS

    def share(k, shift):
        return dot(take(tokens, z + shift), down_weight[k * width : (k + 1) * width], 1, 1)

    chunks = range(CHUNKS)
    far = [send_z_by_core(share(k, 2).astype(BF16)) for k in chunks]
    act_far = send_z_by_core(jnp.where(even, act_below, act_above))

    sides = []
    for k in chunks:
        got = far[k].astype(F32)
        zero = jnp.zeros_like(got)
        up = (share(k, 1) + jnp.where(even, got, zero)).astype(BF16)
        down = (share(k, -1) + jnp.where(even, zero, got)).astype(BF16)
        sides.append((send_z(up, 1), send_z(down, -1)))
    own, near = [], []
    for k in chunks:
        total = share(k, 0) + sides[k][0].astype(F32) + sides[k][1].astype(F32)
        own.append((total * slope[:, k * width : (k + 1) * width]).astype(BF16))
        near.append((send_z(own[k], 1), send_z(own[k], -1)))

    act_all = jnp.zeros((NZ,) + activated.shape, BF16)
    for shift, block in ((0, activated), (-1, act_below), (1, act_above), (2, act_far)):
        act_all = put(act_all, block, z + shift)
    down_grad = dot(act_all.reshape(-1, act_all.shape[2]), cot, 0, 0).astype(BF16)

    last = []
    for k in chunks:
        onward = jnp.where(even, *near[k])
        if k == 0:
            onward = after(onward, down_grad)
        last.append(send_z_by_core(onward))

    hidden = jnp.zeros((NZ,) + preact.shape, BF16)
    plane = jnp.zeros((NY,) + (preact.shape[0], up_weight.shape[0] // 2), BF16)
    for shift, blocks in (
        (0, own),
        (-1, [n[0] for n in near]),
        (1, [n[1] for n in near]),
        (2, last),
    ):
        block = jnp.concatenate(blocks, axis=1)
        hidden = put(hidden, block, z + shift)
        ours, theirs = halves(dot(block, up_weight, 1, 1).astype(BF16), even)
        plane = put(plane, (ours + swap_cores(theirs).astype(F32)).astype(BF16), z + shift)

    plane = plane.reshape(NY, NX, -1, plane.shape[-1])
    line = line_reduce(jnp.where(even, plane, plane.swapaxes(0, 1)), second, 1).astype(BF16)
    up_grad = dot(inputs, hidden.reshape(-1, hidden.shape[2]), 0, 0).astype(BF16)
    pair = line_reduce(after(line, up_grad), first, 0).astype(BF16)
    n = pair.shape[0] // 2
    upper, lower = pair[:n], pair[n:]
    other = swap_cores(jnp.where(even, lower, upper))
    input_grad = ordered(even, jnp.where(even, upper, lower), other, 1)
    return (input_grad, up_grad, down_grad)


def solution(mesh):
    in_specs = (P("row", "col"), P("row", "col"), P("col", "row"), P("col", "row"), P("row", "col"))
    out_specs = (P("row", "col"), P("col", "row"), P("row", "col"))
    return jax.shard_map(local, mesh=mesh, in_specs=in_specs, out_specs=out_specs, check_vma=False)
```

time: 354 us -> 147 us (0.42)
  waiting for transfers between devices: 291 us -> 53.6 us
  starting transfers between devices: 0.24 us -> 55.5 us
  between operations: 14.1 us -> 1.32 us
  matrix products: 36.4 us -> 26.7 us
  local copies, waits for them, and re-layouts: 7.04 us -> 1.95 us
  other arithmetic: 3.67 us -> 8.05 us
    all_gather x4 -> x0, waiting for transfers between devices: 152 us -> none  [the longest x1 50.9 us: local(): lax.all_gather(out_cotangent, 'row', axis=0, tiled=True)]
    reduce_scatter x2 -> x0, waiting for transfers between devices: 137 us -> none  [the longest x1 74 us: local(): lax.psum_scatter(lax.dot_general(hidden_all, up_weight, (((1,), (1,)), ((...]
    ppermute x0 -> x38, starting transfers between devices: none -> 55.5 us  [the longest x8 16.1 us: swap_cores(): return lax.ppermute(v, 'row', SIBLING)]
    ppermute x0 -> x38, waiting for transfers between devices: none -> 53.6 us  [the longest x10 18.4 us: send_z(): return lax.ppermute(v, 'col', z_step(shift))]
    dot_general x4 -> x14, matrix products: 36.4 us -> 26.7 us  [dot(): lax.dot_general(a, b, (((ca,), (cb,)), ((), ())), preferred_element_type=...]
    unnamed x7 -> x11, local copies, waits for them, and re-layouts: 7.04 us -> 0.06 us
    select_n x0 -> x16, other arithmetic: none -> 4.37 us  [the longest x4 2.44 us: ordered(): jnp.where(even, jnp.concatenate([ours, other], axis), jnp.concatenate([ot...]
  transfers between devices with their start and end apart: 6 -> 38, of which waited for: 6 -> 17; matrix products, arithmetic and copies ran while one was open for 10% -> 21% of each run, Pallas kernels for 0% -> 0%
where the time goes in v1:
time: 147 us
  starting transfers between devices  55.5 us (38%)
  waiting for transfers between devices  53.6 us (36%)
  matrix products  26.7 us (18%)
  other arithmetic  8.05 us (5%)
  local copies, waits for them, and re-layouts  1.95 us (1%)
    dot_general x14, matrix products, dot(): lax.dot_general(a, b, (((ca,), (cb,)), ((), ())), preferred_element_type=...  26.7 us
    ppermute x10, waiting for transfers between devices, send_z(): return lax.ppermute(v, 'col', z_step(shift))  18.4 us
    ppermute x5, waiting for transfers between devices, send_z_by_core(): return lax.ppermute(v, ('row', 'col'), Z_BY_CORE)  16.7 us
    ppermute x8, starting transfers between devices, swap_cores(): return lax.ppermute(v, 'row', SIBLING)  16.1 us
    ppermute x9, starting transfers between devices, line_send(): lax.ppermute(v, 'row', plane_step(shift, x_core))  14.3 us
    ppermute x10, starting transfers between devices, send_z(): return lax.ppermute(v, 'col', z_step(shift))  14.2 us
    ppermute x9, waiting for transfers between devices, line_send(): lax.ppermute(v, 'row', plane_step(shift, x_core))  8.65 us
    ppermute x6, waiting for transfers between devices, line_reduce(): lax.ppermute(take(v, place + shift), 'row', plane_step(shift, x_core))  7.05 us
  transfers between devices with their start and end apart: 38, of which 17 were waited for; matrix products, arithmetic and copies ran while one was open for 21% of the time, Pallas kernels for 0%

profile of v1, /device:TPU:1, one launch (start us, length us, event | category | flops | bytes accessed | tf_op | source)
XLA Modules:
  0.0 147.1 jit_solution(4382447430065301874)
XLA Ops:
  0.6 1.0 broadcast_select_fusion.8
  1.6 1.5 %collective-permute-start = (bf16[2,32,768]{2,1,0:T(8,128)(2,1)S(1)}, bf16[2,32,768]{2,1,0:T(8,128)(2,1)S(1)}, u32[]{:S(2)}, u32[]{:S(2)}) collective-permute-start(bf16[2,32,768]{2,1,0:T(8,128)(2,1)S(1)} %get-tuple-element.34), channel_id=1, source_target_pairs={{0,4},{4,0},{8,12},{12,8},{16,20},{20,16},{24,28},{28,24},{32,36},... | collective-permute-start | bytes 294920 | tf_op jit(solution)/shard_map/ppermute | solution.py:45
  3.1 0.9 collective-permute-done
  4.1 1.4 collective-permute-start.1
  5.5 1.5 %collective-permute-start.2 = (bf16[2,64,768]{2,1,0:T(8,128)(2,1)S(1)}, bf16[2,64,768]{2,1,0:T(8,128)(2,1)S(1)}, u32[]{:S(2)}, u32[]{:S(2)}) collective-permute-start(bf16[2,64,768]{2,1,0:T(8,128)(2,1)S(1)} %maximum_select_fusion.4), channel_id=1, source_target_pairs={{0,24},{4,100},{8,0},{12,108},{16,8},{20,116},{24,16},{28,124},{32... | collective-permute-start | bytes 589832 | tf_op jit(solution)/shard_map/ppermute | solution.py:96
  7.1 1.6 %collective-permute-start.3 = (bf16[2,64,768]{2,1,0:T(8,128)(2,1)S(1)}, bf16[2,64,768]{2,1,0:T(8,128)(2,1)S(1)}, u32[]{:S(2)}, u32[]{:S(2)}) collective-permute-start(bf16[2,64,768]{2,1,0:T(8,128)(2,1)S(1)} %maximum_select_fusion.4), channel_id=1, source_target_pairs={{0,16},{4,68},{8,24},{12,76},{16,0},{20,84},{24,8},{28,92},{32,48}... | collective-permute-start | bytes 589832 | tf_op jit(solution)/shard_map/ppermute | solution.py:96
  8.6 2.2 %fusion.11 = (bf16[256,1536]{1,0:T(8,128)(2,1)S(1)}, f32[256,1536]{1,0:T(8,128)S(1)}) fusion(bf16[256,1536]{1,0:T(8,128)(2,1)} %param.7), kind=kLoop, calls=%fused_computation.27 | loop fusion | flops 7864320 | bytes 3145728 | tf_op jit(solution)/shard_map/convert_element_type | solution.py:128
  10.8 1.7 %collective-permute-start.21 = (bf16[256,1536]{1,0:T(8,128)(2,1)S(1)}, bf16[256,1536]{1,0:T(8,128)(2,1)S(1)}, u32[]{:S(2)}, u32[]{:S(2)}) collective-permute-start(bf16[256,1536]{1,0:T(8,128)(2,1)S(1)} %get-tuple-element.16), channel_id=1, source_target_pairs={{0,1},{1,2},{2,3},{3,0},{4,5},{5,6},{6,7},{7,4},{8,9},{9,10},{10,1... | collective-permute-start | bytes 2359304 | tf_op jit(solution)/shard_map/ppermute | solution.py:49
  12.5 2.2 %collective-permute-start.22 = (bf16[256,1536]{1,0:T(8,128)(2,1)S(1)}, bf16[256,1536]{1,0:T(8,128)(2,1)S(1)}, u32[]{:S(2)}, u32[]{:S(2)}) collective-permute-start(bf16[256,1536]{1,0:T(8,128)(2,1)S(1)} %get-tuple-element.16), channel_id=1, source_target_pairs={{0,3},{1,0},{2,1},{3,2},{4,7},{5,4},{6,5},{7,6},{8,11},{9,8},{10,9... | collective-permute-start | bytes 2359304 | tf_op jit(solution)/shard_map/ppermute | solution.py:49
  15.0 0.6 bitcast_dynamic-update-slice_fusion.7
  15.8 1.3 collective-permute-start.4
  17.1 1.5 collective-permute-start.5
  18.5 1.5 %collective-permute-start.6 = (bf16[4,64,768]{2,1,0:T(8,128)(2,1)S(1)}, bf16[4,64,768]{2,1,0:T(8,128)(2,1)S(1)}, u32[]{:S(2)}, u32[]{:S(2)}) collective-permute-start(bf16[4,64,768]{2,1,0:T(8,128)(2,1)S(1)} %get-tuple-element.28), channel_id=1, source_target_pairs={{0,64},{4,20},{8,72},{12,28},{16,80},{20,4},{24,88},{28,12},{32,96... | collective-permute-start | bytes 1179656 | tf_op jit(solution)/shard_map/ppermute | solution.py:96
  20.5 3.5 %collective-permute-done.4 = bf16[4,64,768]{2,1,0:T(8,128)(2,1)S(1)} collective-permute-done((bf16[4,64,768]{2,1,0:T(8,128)(2,1)S(1)}, bf16[4,64,768]{2,1,0:T(8,128)(2,1)S(1)}, u32[]{:S(2)}, u32[]{:S(2)}) %collective-permute-start.4) | collective-permute-done | bytes 393248 | tf_op jit(solution)/shard_map/ppermute | solution.py:96
  24.1 5.1 %collective-permute-done.6 = bf16[4,64,768]{2,1,0:T(8,128)(2,1)S(1)} collective-permute-done((bf16[4,64,768]{2,1,0:T(8,128)(2,1)S(1)}, bf16[4,64,768]{2,1,0:T(8,128)(2,1)S(1)}, u32[]{:S(2)}, u32[]{:S(2)}) %collective-permute-start.6) | collective-permute-done | bytes 393248 | tf_op jit(solution)/shard_map/ppermute | solution.py:96
  29.4 2.5 %collective-permute-start.7 = (bf16[1024,768]{1,0:T(8,128)(2,1)S(1)}, bf16[1024,768]{1,0:T(8,128)(2,1)S(1)}, u32[]{:S(2)}, u32[]{:S(2)}) collective-permute-start(bf16[1024,768]{1,0:T(8,128)(2,1)S(1)} %bitcast.127), channel_id=1, source_target_pairs={{0,4},{4,0},{8,12},{12,8},{16,20},{20,16},{24,28},{28,24},{32,36},... | collective-permute-start | bytes 4718600 | tf_op jit(solution)/shard_map/ppermute | solution.py:45
  32.0 2.1 %collective-permute-start.23 = (bf16[256,1536]{1,0:T(8,128)(2,1)S(1)}, bf16[256,1536]{1,0:T(8,128)(2,1)S(1)}, u32[]{:S(2)}, u32[]{:S(2)}) collective-permute-start(bf16[256,1536]{1,0:T(8,128)(2,1)S(1)} %broadcast_select_fusion), channel_id=1, source_target_pairs={{0,1},{1,2},{2,3},{3,0},{4,7},{5,4},{6,5},{7,6},{8,9},{9,10},{10,1... | collective-permute-start | bytes 2359304 | tf_op jit(solution)/shard_map/ppermute | solution.py:53
  34.2 9.0 %collective-permute-done.23 = bf16[256,1536]{1,0:T(8,128)(2,1)S(1)} collective-permute-done((bf16[256,1536]{1,0:T(8,128)(2,1)S(1)}, bf16[256,1536]{1,0:T(8,128)(2,1)S(1)}, u32[]{:S(2)}, u32[]{:S(2)}) %collective-permute-start.23) | collective-permute-done | bytes 786464 | tf_op jit(solution)/shard_map/ppermute | solution.py:53
  43.3 0.9 maximum_select_fusion
  44.2 0.8 fusion.82
  45.0 0.8 fusion.79
  45.8 0.9 maximum_select_fusion.1
  46.7 2.1 %collective-permute-start.30 = (bf16[4,64,768]{2,1,0:T(8,128)(2,1)S(1)}, bf16[4,64,768]{2,1,0:T(8,128)(2,1)S(1)}, u32[]{:S(2)}, u32[]{:S(2)}) collective-permute-start(bf16[4,64,768]{2,1,0:T(8,128)(2,1)S(1)} %get-tuple-element.11), channel_id=1, source_target_pairs={{0,32},{4,12},{8,40},{12,20},{16,48},{20,28},{24,56},{28,4},{32,64... | collective-permute-start | bytes 1179656 | tf_op jit(solution)/shard_map/ppermute | solution.py:96
  48.8 1.6 %collective-permute-start.31 = (bf16[4,64,768]{2,1,0:T(8,128)(2,1)S(1)}, bf16[4,64,768]{2,1,0:T(8,128)(2,1)S(1)}, u32[]{:S(2)}, u32[]{:S(2)}) collective-permute-start(bf16[4,64,768]{2,1,0:T(8,128)(2,1)S(1)} %get-tuple-element.11), channel_id=1, source_target_pairs={{0,96},{4,28},{8,104},{12,4},{16,112},{20,12},{24,120},{28,20},{32... | collective-permute-start | bytes 1179656 | tf_op jit(solution)/shard_map/ppermute | solution.py:96
  50.4 1.7 %collective-permute-start.32 = (bf16[4,64,768]{2,1,0:T(8,128)(2,1)S(1)}, bf16[4,64,768]{2,1,0:T(8,128)(2,1)S(1)}, u32[]{:S(2)}, u32[]{:S(2)}) collective-permute-start(bf16[4,64,768]{2,1,0:T(8,128)(2,1)S(1)} %get-tuple-element.11), channel_id=1, source_target_pairs={{0,64},{4,20},{8,72},{12,28},{16,80},{20,4},{24,88},{28,12},{32,96... | collective-permute-start | bytes 1179656 | tf_op jit(solution)/shard_map/ppermute | solution.py:96
  52.2 3.1 %collective-permute-start.11 = (bf16[256,768]{1,0:T(8,128)(2,1)S(1)}, bf16[256,768]{1,0:T(8,128)(2,1)S(1)}, u32[]{:S(2)}, u32[]{:S(2)}) collective-permute-start(bf16[256,768]{1,0:T(8,128)(2,1)S(1)} %fusion.82), channel_id=1, source_target_pairs={{0,1},{1,2},{2,3},{3,0},{4,7},{5,4},{6,5},{7,6},{8,9},{9,10},{10,1... | collective-permute-start | bytes 1179656 | tf_op jit(solution)/shard_map/ppermute | solution.py:53
  55.3 6.8 %convolution_convert_fusion.1 = bf16[1536,1536]{1,0:T(8,128)(2,1)} fusion(bf16[1024,1536]{1,0:T(8,128)(2,1)S(1)} %bitcast.131, bf16[1024,1536]{1,0:T(8,128)(2,1)S(1)} %maximum_select_fusion.1), kind=kOutput, calls=%fused_computation.1 | convolution fusion | flops 4834197504 | bytes 11010048 | tf_op jit(solution)/shard_map/dot_general | solution.py:57
  62.1 0.8 fusion.61
  62.9 1.4 collective-permute-start.13
  64.3 0.8 fusion.64
  65.3 0.8 fusion.70
  66.2 0.8 fusion.73
  67.0 2.6 %collective-permute-start.10 = (bf16[256,768]{1,0:T(8,128)(2,1)S(1)}, bf16[256,768]{1,0:T(8,128)(2,1)S(1)}, u32[]{:S(2)}, u32[]{:S(2)}) collective-permute-start(bf16[256,768]{1,0:T(8,128)(2,1)S(1)} %fusion.70), channel_id=1, source_target_pairs={{0,3},{1,0},{2,1},{3,2},{4,7},{5,4},{6,5},{7,6},{8,11},{9,8},{10,9... | collective-permute-start | bytes 1179656 | tf_op jit(solution)/shard_map/ppermute | solution.py:49
  70.1 2.4 %collective-permute-start.33 = (bf16[1024,768]{1,0:T(8,128)(2,1)S(1)}, bf16[1024,768]{1,0:T(8,128)(2,1)S(1)}, u32[]{:S(2)}, u32[]{:S(2)}) collective-permute-start(bf16[1024,768]{1,0:T(8,128)(2,1)S(1)} %bitcast.133), channel_id=1, source_target_pairs={{0,4},{4,0},{8,12},{12,8},{16,20},{20,16},{24,28},{28,24},{32,36},... | collective-permute-start | bytes 4718600 | tf_op jit(solution)/shard_map/ppermute | solution.py:45
  72.5 0.5 collective-permute-done.13
  73.0 2.2 %collective-permute-done.12 = bf16[256,768]{1,0:T(8,128)(2,1)S(1)} collective-permute-done((bf16[256,768]{1,0:T(8,128)(2,1)S(1)}, bf16[256,768]{1,0:T(8,128)(2,1)S(1)}, u32[]{:S(2)}, u32[]{:S(2)}) %collective-permute-start.12) | collective-permute-done | bytes 393248 | tf_op jit(solution)/shard_map/ppermute | solution.py:49
  75.2 0.9 fusion.67
  76.2 3.0 %collective-permute-start.19 = (bf16[256,768]{1,0:T(8,128)(2,1)S(1)}, bf16[256,768]{1,0:T(8,128)(2,1)S(1)}, u32[]{:S(2)}, u32[]{:S(2)}) collective-permute-start(bf16[256,768]{1,0:T(8,128)(2,1)S(1)} %fusion.67), channel_id=1, source_target_pairs={{0,3},{1,0},{2,1},{3,2},{4,7},{5,4},{6,5},{7,6},{8,11},{9,8},{10,9... | collective-permute-start | bytes 1179656 | tf_op jit(solution)/shard_map/ppermute | solution.py:49
  79.1 2.3 %collective-permute-done.10 = bf16[256,768]{1,0:T(8,128)(2,1)S(1)} collective-permute-done((bf16[256,768]{1,0:T(8,128)(2,1)S(1)}, bf16[256,768]{1,0:T(8,128)(2,1)S(1)}, u32[]{:S(2)}, u32[]{:S(2)}) %collective-permute-start.10) | collective-permute-done | bytes 393248 | tf_op jit(solution)/shard_map/ppermute | solution.py:49
  81.4 2.2 %collective-permute-done.9 = bf16[256,768]{1,0:T(8,128)(2,1)S(1)} collective-permute-done((bf16[256,768]{1,0:T(8,128)(2,1)S(1)}, bf16[256,768]{1,0:T(8,128)(2,1)S(1)}, u32[]{:S(2)}, u32[]{:S(2)}) %collective-permute-start.9) | collective-permute-done | bytes 393248 | tf_op jit(solution)/shard_map/ppermute | solution.py:49
  83.6 0.8 fusion.76
  84.6 3.0 %collective-permute-start.18 = (bf16[256,768]{1,0:T(8,128)(2,1)S(1)}, bf16[256,768]{1,0:T(8,128)(2,1)S(1)}, u32[]{:S(2)}, u32[]{:S(2)}) collective-permute-start(bf16[256,768]{1,0:T(8,128)(2,1)S(1)} %fusion.76), channel_id=1, source_target_pairs={{0,3},{1,0},{2,1},{3,2},{4,7},{5,4},{6,5},{7,6},{8,11},{9,8},{10,9... | collective-permute-start | bytes 1179656 | tf_op jit(solution)/shard_map/ppermute | solution.py:49
  87.6 1.4 convolution_convert_fusion.5
  89.3 11.2 %collective-permute-done.15 = bf16[256,768]{1,0:T(8,128)(2,1)S(1)} collective-permute-done((bf16[256,768]{1,0:T(8,128)(2,1)S(1)}, bf16[256,768]{1,0:T(8,128)(2,1)S(1)}, u32[]{:S(2)}, u32[]{:S(2)}) %collective-permute-start.15) | collective-permute-done | bytes 393248 | tf_op jit(solution)/shard_map/ppermute | solution.py:49
  100.5 2.7 %collective-permute-start.14 = (bf16[256,768]{1,0:T(8,128)(2,1)S(1)}, bf16[256,768]{1,0:T(8,128)(2,1)S(1)}, u32[]{:S(2)}, u32[]{:S(2)}) collective-permute-start(bf16[256,768]{1,0:T(8,128)(2,1)S(1)} %broadcast_select_fusion.6), channel_id=1, source_target_pairs={{0,4},{4,0},{8,12},{12,8},{16,20},{20,16},{24,28},{28,24},{32,36},... | collective-permute-start | bytes 1179656 | tf_op jit(solution)/shard_map/ppermute | solution.py:45
  103.5 1.4 convolution_convert_fusion.4
  105.1 1.0 collective-permute-start.24
  106.3 1.4 convolution_convert_fusion.3
  108.4 3.6 %collective-permute-done.24 = bf16[256,768]{1,0:T(8,128)(2,1)S(1)} collective-permute-done((bf16[256,768]{1,0:T(8,128)(2,1)S(1)}, bf16[256,768]{1,0:T(8,128)(2,1)S(1)}, u32[]{:S(2)}, u32[]{:S(2)}) %collective-permute-start.24) | collective-permute-done | bytes 393248 | tf_op jit(solution)/shard_map/ppermute | solution.py:53
  112.1 4.2 %collective-permute-done.25 = bf16[256,768]{1,0:T(8,128)(2,1)S(1)} collective-permute-done((bf16[256,768]{1,0:T(8,128)(2,1)S(1)}, bf16[256,768]{1,0:T(8,128)(2,1)S(1)}, u32[]{:S(2)}, u32[]{:S(2)}) %collective-permute-start.25) | collective-permute-done | bytes 393248 | tf_op jit(solution)/shard_map/ppermute | solution.py:53
  116.3 1.4 convolution_convert_fusion.2
  117.8 2.6 %collective-permute-start.26 = (bf16[256,768]{1,0:T(8,128)(2,1)S(1)}, bf16[256,768]{1,0:T(8,128)(2,1)S(1)}, u32[]{:S(2)}, u32[]{:S(2)}) collective-permute-start(bf16[256,768]{1,0:T(8,128)(2,1)S(1)} %broadcast_select_fusion.1), channel_id=1, source_target_pairs={{0,4},{4,0},{8,12},{12,8},{16,20},{20,16},{24,28},{28,24},{32,36},... | collective-permute-start | bytes 1179656 | tf_op jit(solution)/shard_map/ppermute | solution.py:45
  120.7 1.0 collective-permute-done.26
  122.1 1.3 collective-permute-start.29
  123.4 1.4 collective-permute-start.28
  124.9 7.7 %convolution_convert_fusion = bf16[1536,1536]{1,0:T(8,128)(2,1)} fusion(bf16[1024,1536]{1,0:T(8,128)(2,1)S(1)} %bitcast.132, bf16[1024,768]{1,0:T(8,128)(2,1)S(1)} %collective-permute-done.33, bf16[1024,768]{1,0:T(8,128)(2,1)S(1)} %bitcast.134, pred[]{:T(512)S(6)} %eq.50), kind=kOutput, calls=%fused_computation | convolution fusion | flops 4848353280 | bytes 11010049 | tf_op jit(solution)/shard_map/dot_general | solution.py:57
  132.6 0.5 collective-permute-done.28
  133.1 1.7 %collective-permute-done.27 = bf16[4,64,768]{2,1,0:T(8,128)(2,1)S(1)} collective-permute-done((bf16[4,64,768]{2,1,0:T(8,128)(2,1)S(1)}, bf16[4,64,768]{2,1,0:T(8,128)(2,1)S(1)}, u32[]{:S(2)}, u32[]{:S(2)}) %collective-permute-start.27) | collective-permute-done | bytes 393248 | tf_op jit(solution)/shard_map/ppermute | solution.py:108
  135.2 1.4 collective-permute-start.35
  136.7 3.4 %collective-permute-done.36 = bf16[64,768]{1,0:T(8,128)(2,1)S(1)} collective-permute-done((bf16[64,768]{1,0:T(8,128)(2,1)S(1)}, bf16[64,768]{1,0:T(8,128)(2,1)S(1)}, u32[]{:S(2)}, u32[]{:S(2)}) %collective-permute-start.36) | collective-permute-done | bytes 98336 | tf_op jit(solution)/shard_map/ppermute | solution.py:108
  140.1 1.4 collective-permute-done.34
  141.6 3.9 %collective-permute-start.37 = (bf16[32,768]{1,0:T(8,128)(2,1)S(1)}, bf16[32,768]{1,0:T(8,128)(2,1)S(1)}, u32[]{:S(2)}, u32[]{:S(2)}) collective-permute-start(bf16[32,768]{1,0:T(8,128)(2,1)S(1)} %get-tuple-element.36), channel_id=1, source_target_pairs={{0,4},{4,0},{8,12},{12,8},{16,20},{20,16},{24,28},{28,24},{32,36},... | collective-permute-start | bytes 147464 | tf_op jit(solution)/shard_map/ppermute | solution.py:45
  145.5 0.9 collective-permute-done.37
  146.4 0.7 maximum_select_fusion.5
  (94 shorter events, 5.3 us)
Async XLA Ops:
  1.6 2.4 %collective-permute-start = (bf16[2,32,768]{2,1,0:T(8,128)(2,1)S(1)}, bf16[2,32,768]{2,1,0:T(8,128)(2,1)S(1)}, u32[]{:S(2)}, u32[]{:S(2)}) collective-permute-start(bf16[2,32,768]{2,1,0:T(8,128)(2,1)S(1)} %get-tuple-element.34), channel_id=1, source_target_pairs={{0,4},{4,0},{8,12},{12,8},{16,20},{20,16},{24,28},{28,24},{32,36},... | collective-permute-start | bytes 294920 | tf_op jit(solution)/shard_map/ppermute | solution.py:45
  4.1 11.6 %collective-permute-start.1 = (bf16[2,64,768]{2,1,0:T(8,128)(2,1)S(1)}, bf16[2,64,768]{2,1,0:T(8,128)(2,1)S(1)}, u32[]{:S(2)}, u32[]{:S(2)}) collective-permute-start(bf16[2,64,768]{2,1,0:T(8,128)(2,1)S(1)} %maximum_select_fusion.4), channel_id=1, source_target_pairs={{0,8},{4,36},{8,16},{12,44},{16,24},{20,52},{24,0},{28,60},{32,40}... | collective-permute-start | bytes 589832 | tf_op jit(solution)/shard_map/ppermute | solution.py:96
  5.5 10.2 %collective-permute-start.2 = (bf16[2,64,768]{2,1,0:T(8,128)(2,1)S(1)}, bf16[2,64,768]{2,1,0:T(8,128)(2,1)S(1)}, u32[]{:S(2)}, u32[]{:S(2)}) collective-permute-start(bf16[2,64,768]{2,1,0:T(8,128)(2,1)S(1)} %maximum_select_fusion.4), channel_id=1, source_target_pairs={{0,24},{4,100},{8,0},{12,108},{16,8},{20,116},{24,16},{28,124},{32... | collective-permute-start | bytes 589832 | tf_op jit(solution)/shard_map/ppermute | solution.py:96
  7.1 8.7 %collective-permute-start.3 = (bf16[2,64,768]{2,1,0:T(8,128)(2,1)S(1)}, bf16[2,64,768]{2,1,0:T(8,128)(2,1)S(1)}, u32[]{:S(2)}, u32[]{:S(2)}) collective-permute-start(bf16[2,64,768]{2,1,0:T(8,128)(2,1)S(1)} %maximum_select_fusion.4), channel_id=1, source_target_pairs={{0,16},{4,68},{8,24},{12,76},{16,0},{20,84},{24,8},{28,92},{32,48}... | collective-permute-start | bytes 589832 | tf_op jit(solution)/shard_map/ppermute | solution.py:96
  10.8 4.2 %copy-start = (bf16[256,1536]{1,0:T(8,128)(2,1)S(1)}, bf16[256,1536]{1,0:T(8,128)(2,1)}, u32[]{:S(2)}) copy-start(bf16[256,1536]{1,0:T(8,128)(2,1)} %param.7) | copy-start | bytes 2359300
  10.8 21.1 %collective-permute-start.21 = (bf16[256,1536]{1,0:T(8,128)(2,1)S(1)}, bf16[256,1536]{1,0:T(8,128)(2,1)S(1)}, u32[]{:S(2)}, u32[]{:S(2)}) collective-permute-start(bf16[256,1536]{1,0:T(8,128)(2,1)S(1)} %get-tuple-element.16), channel_id=1, source_target_pairs={{0,1},{1,2},{2,3},{3,0},{4,5},{5,6},{6,7},{7,4},{8,9},{9,10},{10,1... | collective-permute-start | bytes 2359304 | tf_op jit(solution)/shard_map/ppermute | solution.py:49
  12.5 19.4 %collective-permute-start.22 = (bf16[256,1536]{1,0:T(8,128)(2,1)S(1)}, bf16[256,1536]{1,0:T(8,128)(2,1)S(1)}, u32[]{:S(2)}, u32[]{:S(2)}) collective-permute-start(bf16[256,1536]{1,0:T(8,128)(2,1)S(1)} %get-tuple-element.16), channel_id=1, source_target_pairs={{0,3},{1,0},{2,1},{3,2},{4,7},{5,4},{6,5},{7,6},{8,11},{9,8},{10,9... | collective-permute-start | bytes 2359304 | tf_op jit(solution)/shard_map/ppermute | solution.py:49
  15.8 8.2 %collective-permute-start.4 = (bf16[4,64,768]{2,1,0:T(8,128)(2,1)S(1)}, bf16[4,64,768]{2,1,0:T(8,128)(2,1)S(1)}, u32[]{:S(2)}, u32[]{:S(2)}) collective-permute-start(bf16[4,64,768]{2,1,0:T(8,128)(2,1)S(1)} %get-tuple-element.28), channel_id=1, source_target_pairs={{0,32},{4,12},{8,40},{12,20},{16,48},{20,28},{24,56},{28,4},{32,64... | collective-permute-start | bytes 1179656 | tf_op jit(solution)/shard_map/ppermute | solution.py:96
  17.1 7.0 %collective-permute-start.5 = (bf16[4,64,768]{2,1,0:T(8,128)(2,1)S(1)}, bf16[4,64,768]{2,1,0:T(8,128)(2,1)S(1)}, u32[]{:S(2)}, u32[]{:S(2)}) collective-permute-start(bf16[4,64,768]{2,1,0:T(8,128)(2,1)S(1)} %get-tuple-element.28), channel_id=1, source_target_pairs={{0,96},{4,28},{8,104},{12,4},{16,112},{20,12},{24,120},{28,20},{32... | collective-permute-start | bytes 1179656 | tf_op jit(solution)/shard_map/ppermute | solution.py:96
  18.5 10.7 %collective-permute-start.6 = (bf16[4,64,768]{2,1,0:T(8,128)(2,1)S(1)}, bf16[4,64,768]{2,1,0:T(8,128)(2,1)S(1)}, u32[]{:S(2)}, u32[]{:S(2)}) collective-permute-start(bf16[4,64,768]{2,1,0:T(8,128)(2,1)S(1)} %get-tuple-element.28), channel_id=1, source_target_pairs={{0,64},{4,20},{8,72},{12,28},{16,80},{20,4},{24,88},{28,12},{32,96... | collective-permute-start | bytes 1179656 | tf_op jit(solution)/shard_map/ppermute | solution.py:96
  29.4 13.9 %collective-permute-start.7 = (bf16[1024,768]{1,0:T(8,128)(2,1)S(1)}, bf16[1024,768]{1,0:T(8,128)(2,1)S(1)}, u32[]{:S(2)}, u32[]{:S(2)}) collective-permute-start(bf16[1024,768]{1,0:T(8,128)(2,1)S(1)} %bitcast.127), channel_id=1, source_target_pairs={{0,4},{4,0},{8,12},{12,8},{16,20},{20,16},{24,28},{28,24},{32,36},... | collective-permute-start | bytes 4718600 | tf_op jit(solution)/shard_map/ppermute | solution.py:45
  31.9 12.2 %slice-start = ((s8[4718592]{0:T(1024)(128)(4,1)}), s8[4194304]{0:T(1024)(128)(4,1)S(1)}, s32[]{:S(2)}) async-start(s8[4718592]{0:T(1024)(128)(4,1)} %bitcast.137), calls=%async_computation | async-start | bytes 8388608
  32.0 11.2 %collective-permute-start.23 = (bf16[256,1536]{1,0:T(8,128)(2,1)S(1)}, bf16[256,1536]{1,0:T(8,128)(2,1)S(1)}, u32[]{:S(2)}, u32[]{:S(2)}) collective-permute-start(bf16[256,1536]{1,0:T(8,128)(2,1)S(1)} %broadcast_select_fusion), channel_id=1, source_target_pairs={{0,1},{1,2},{2,3},{3,0},{4,7},{5,4},{6,5},{7,6},{8,9},{9,10},{10,1... | collective-permute-start | bytes 2359304 | tf_op jit(solution)/shard_map/ppermute | solution.py:53
  34.2 9.9 %slice-start.1 = ((s8[4718592]{0:T(1024)(128)(4,1)}), s8[524288]{0:T(1024)(128)(4,1)S(1)}, s32[]{:S(2)}) async-start(s8[4718592]{0:T(1024)(128)(4,1)} %bitcast.137), calls=%async_computation.1 | async-start | bytes 1048576
  46.7 20.3 %collective-permute-start.30 = (bf16[4,64,768]{2,1,0:T(8,128)(2,1)S(1)}, bf16[4,64,768]{2,1,0:T(8,128)(2,1)S(1)}, u32[]{:S(2)}, u32[]{:S(2)}) collective-permute-start(bf16[4,64,768]{2,1,0:T(8,128)(2,1)S(1)} %get-tuple-element.11), channel_id=1, source_target_pairs={{0,32},{4,12},{8,40},{12,20},{16,48},{20,28},{24,56},{28,4},{32,64... | collective-permute-start | bytes 1179656 | tf_op jit(solution)/shard_map/ppermute | solution.py:96
  48.8 20.8 %collective-permute-start.31 = (bf16[4,64,768]{2,1,0:T(8,128)(2,1)S(1)}, bf16[4,64,768]{2,1,0:T(8,128)(2,1)S(1)}, u32[]{:S(2)}, u32[]{:S(2)}) collective-permute-start(bf16[4,64,768]{2,1,0:T(8,128)(2,1)S(1)} %get-tuple-element.11), channel_id=1, source_target_pairs={{0,96},{4,28},{8,104},{12,4},{16,112},{20,12},{24,120},{28,20},{32... | collective-permute-start | bytes 1179656 | tf_op jit(solution)/shard_map/ppermute | solution.py:96
  50.4 19.3 %collective-permute-start.32 = (bf16[4,64,768]{2,1,0:T(8,128)(2,1)S(1)}, bf16[4,64,768]{2,1,0:T(8,128)(2,1)S(1)}, u32[]{:S(2)}, u32[]{:S(2)}) collective-permute-start(bf16[4,64,768]{2,1,0:T(8,128)(2,1)S(1)} %get-tuple-element.11), channel_id=1, source_target_pairs={{0,64},{4,20},{8,72},{12,28},{16,80},{20,4},{24,88},{28,12},{32,96... | collective-permute-start | bytes 1179656 | tf_op jit(solution)/shard_map/ppermute | solution.py:96
  52.2 9.9 %collective-permute-start.11 = (bf16[256,768]{1,0:T(8,128)(2,1)S(1)}, bf16[256,768]{1,0:T(8,128)(2,1)S(1)}, u32[]{:S(2)}, u32[]{:S(2)}) collective-permute-start(bf16[256,768]{1,0:T(8,128)(2,1)S(1)} %fusion.82), channel_id=1, source_target_pairs={{0,1},{1,2},{2,3},{3,0},{4,7},{5,4},{6,5},{7,6},{8,9},{9,10},{10,1... | collective-permute-start | bytes 1179656 | tf_op jit(solution)/shard_map/ppermute | solution.py:53
  55.3 9.8 %collective-permute-start.8 = (bf16[256,768]{1,0:T(8,128)(2,1)S(1)}, bf16[256,768]{1,0:T(8,128)(2,1)S(1)}, u32[]{:S(2)}, u32[]{:S(2)}) collective-permute-start(bf16[256,768]{1,0:T(8,128)(2,1)S(1)} %fusion.79), channel_id=1, source_target_pairs={{0,1},{1,2},{2,3},{3,0},{4,7},{5,4},{6,5},{7,6},{8,9},{9,10},{10,1... | collective-permute-start | bytes 1179656 | tf_op jit(solution)/shard_map/ppermute | solution.py:53
  62.9 10.1 %collective-permute-start.13 = (bf16[256,768]{1,0:T(8,128)(2,1)S(1)}, bf16[256,768]{1,0:T(8,128)(2,1)S(1)}, u32[]{:S(2)}, u32[]{:S(2)}) collective-permute-start(bf16[256,768]{1,0:T(8,128)(2,1)S(1)} %fusion.61), channel_id=1, source_target_pairs={{0,3},{1,0},{2,1},{3,2},{4,7},{5,4},{6,5},{7,6},{8,11},{9,8},{10,9... | collective-permute-start | bytes 1179656 | tf_op jit(solution)/shard_map/ppermute | solution.py:49
  65.1 10.1 %collective-permute-start.12 = (bf16[256,768]{1,0:T(8,128)(2,1)S(1)}, bf16[256,768]{1,0:T(8,128)(2,1)S(1)}, u32[]{:S(2)}, u32[]{:S(2)}) collective-permute-start(bf16[256,768]{1,0:T(8,128)(2,1)S(1)} %fusion.64), channel_id=1, source_target_pairs={{0,1},{1,2},{2,3},{3,0},{4,5},{5,6},{6,7},{7,4},{8,9},{9,10},{10,1... | collective-permute-start | bytes 1179656 | tf_op jit(solution)/shard_map/ppermute | solution.py:49
  67.0 14.4 %collective-permute-start.10 = (bf16[256,768]{1,0:T(8,128)(2,1)S(1)}, bf16[256,768]{1,0:T(8,128)(2,1)S(1)}, u32[]{:S(2)}, u32[]{:S(2)}) collective-permute-start(bf16[256,768]{1,0:T(8,128)(2,1)S(1)} %fusion.70), channel_id=1, source_target_pairs={{0,3},{1,0},{2,1},{3,2},{4,7},{5,4},{6,5},{7,6},{8,11},{9,8},{10,9... | collective-permute-start | bytes 1179656 | tf_op jit(solution)/shard_map/ppermute | solution.py:49
  69.6 14.0 %collective-permute-start.9 = (bf16[256,768]{1,0:T(8,128)(2,1)S(1)}, bf16[256,768]{1,0:T(8,128)(2,1)S(1)}, u32[]{:S(2)}, u32[]{:S(2)}) collective-permute-start(bf16[256,768]{1,0:T(8,128)(2,1)S(1)} %fusion.73), channel_id=1, source_target_pairs={{0,1},{1,2},{2,3},{3,0},{4,5},{5,6},{6,7},{7,4},{8,9},{9,10},{10,1... | collective-permute-start | bytes 1179656 | tf_op jit(solution)/shard_map/ppermute | solution.py:49
  69.9 17.6 %slice-start.2 = ((s8[4718592]{0:T(1024)(128)(4,1)}), s8[4194304]{0:T(1024)(128)(4,1)S(1)}, s32[]{:S(2)}) async-start(s8[4718592]{0:T(1024)(128)(4,1)} %bitcast.139), calls=%async_computation.2 | async-start | bytes 8388608
  70.1 17.5 %slice-start.3 = ((s8[4718592]{0:T(1024)(128)(4,1)}), s8[524288]{0:T(1024)(128)(4,1)S(1)}, s32[]{:S(2)}) async-start(s8[4718592]{0:T(1024)(128)(4,1)} %bitcast.139), calls=%async_computation.3 | async-start | bytes 1048576
  70.1 54.8 %collective-permute-start.33 = (bf16[1024,768]{1,0:T(8,128)(2,1)S(1)}, bf16[1024,768]{1,0:T(8,128)(2,1)S(1)}, u32[]{:S(2)}, u32[]{:S(2)}) collective-permute-start(bf16[1024,768]{1,0:T(8,128)(2,1)S(1)} %bitcast.133), channel_id=1, source_target_pairs={{0,4},{4,0},{8,12},{12,8},{16,20},{20,16},{24,28},{28,24},{32,36},... | collective-permute-start | bytes 4718600 | tf_op jit(solution)/shard_map/ppermute | solution.py:45
  76.1 27.3 %collective-permute-start.16 = (bf16[256,768]{1,0:T(8,128)(2,1)S(1)}, bf16[256,768]{1,0:T(8,128)(2,1)S(1)}, u32[]{:S(2)}, u32[]{:S(2)}) collective-permute-start(bf16[256,768]{1,0:T(8,128)(2,1)S(1)} %fusion.67), channel_id=1, source_target_pairs={{0,1},{1,2},{2,3},{3,0},{4,5},{5,6},{6,7},{7,4},{8,9},{9,10},{10,1... | collective-permute-start | bytes 1179656 | tf_op jit(solution)/shard_map/ppermute | solution.py:49
  76.2 27.2 %collective-permute-start.19 = (bf16[256,768]{1,0:T(8,128)(2,1)S(1)}, bf16[256,768]{1,0:T(8,128)(2,1)S(1)}, u32[]{:S(2)}, u32[]{:S(2)}) collective-permute-start(bf16[256,768]{1,0:T(8,128)(2,1)S(1)} %fusion.67), channel_id=1, source_target_pairs={{0,3},{1,0},{2,1},{3,2},{4,7},{5,4},{6,5},{7,6},{8,11},{9,8},{10,9... | collective-permute-start | bytes 1179656 | tf_op jit(solution)/shard_map/ppermute | solution.py:49
  84.5 16.0 %collective-permute-start.15 = (bf16[256,768]{1,0:T(8,128)(2,1)S(1)}, bf16[256,768]{1,0:T(8,128)(2,1)S(1)}, u32[]{:S(2)}, u32[]{:S(2)}) collective-permute-start(bf16[256,768]{1,0:T(8,128)(2,1)S(1)} %fusion.76), channel_id=1, source_target_pairs={{0,1},{1,2},{2,3},{3,0},{4,5},{5,6},{6,7},{7,4},{8,9},{9,10},{10,1... | collective-permute-start | bytes 1179656 | tf_op jit(solution)/shard_map/ppermute | solution.py:49
  84.6 18.6 %collective-permute-start.18 = (bf16[256,768]{1,0:T(8,128)(2,1)S(1)}, bf16[256,768]{1,0:T(8,128)(2,1)S(1)}, u32[]{:S(2)}, u32[]{:S(2)}) collective-permute-start(bf16[256,768]{1,0:T(8,128)(2,1)S(1)} %fusion.76), channel_id=1, source_target_pairs={{0,3},{1,0},{2,1},{3,2},{4,7},{5,4},{6,5},{7,6},{8,11},{9,8},{10,9... | collective-permute-start | bytes 1179656 | tf_op jit(solution)/shard_map/ppermute | solution.py:49
  100.5 7.2 %collective-permute-start.14 = (bf16[256,768]{1,0:T(8,128)(2,1)S(1)}, bf16[256,768]{1,0:T(8,128)(2,1)S(1)}, u32[]{:S(2)}, u32[]{:S(2)}) collective-permute-start(bf16[256,768]{1,0:T(8,128)(2,1)S(1)} %broadcast_select_fusion.6), channel_id=1, source_target_pairs={{0,4},{4,0},{8,12},{12,8},{16,20},{20,16},{24,28},{28,24},{32,36},... | collective-permute-start | bytes 1179656 | tf_op jit(solution)/shard_map/ppermute | solution.py:45
  105.0 15.4 %collective-permute-start.17 = (bf16[256,768]{1,0:T(8,128)(2,1)S(1)}, bf16[256,768]{1,0:T(8,128)(2,1)S(1)}, u32[]{:S(2)}, u32[]{:S(2)}) collective-permute-start(bf16[256,768]{1,0:T(8,128)(2,1)S(1)} %broadcast_select_fusion.5), channel_id=1, source_target_pairs={{0,4},{4,0},{8,12},{12,8},{16,20},{20,16},{24,28},{28,24},{32,36},... | collective-permute-start | bytes 1179656 | tf_op jit(solution)/shard_map/ppermute | solution.py:45
  105.1 7.0 %collective-permute-start.24 = (bf16[256,768]{1,0:T(8,128)(2,1)S(1)}, bf16[256,768]{1,0:T(8,128)(2,1)S(1)}, u32[]{:S(2)}, u32[]{:S(2)}) collective-permute-start(bf16[256,768]{1,0:T(8,128)(2,1)S(1)} %get-tuple-element.10), channel_id=1, source_target_pairs={{0,1},{1,2},{2,3},{3,0},{4,7},{5,4},{6,5},{7,6},{8,9},{9,10},{10,1... | collective-permute-start | bytes 1179656 | tf_op jit(solution)/shard_map/ppermute | solution.py:53
  106.1 10.2 %collective-permute-start.25 = (bf16[256,768]{1,0:T(8,128)(2,1)S(1)}, bf16[256,768]{1,0:T(8,128)(2,1)S(1)}, u32[]{:S(2)}, u32[]{:S(2)}) collective-permute-start(bf16[256,768]{1,0:T(8,128)(2,1)S(1)} %get-tuple-element.21), channel_id=1, source_target_pairs={{0,1},{1,2},{2,3},{3,0},{4,7},{5,4},{6,5},{7,6},{8,9},{9,10},{10,1... | collective-permute-start | bytes 1179656 | tf_op jit(solution)/shard_map/ppermute | solution.py:53
  107.8 12.7 %collective-permute-start.20 = (bf16[256,768]{1,0:T(8,128)(2,1)S(1)}, bf16[256,768]{1,0:T(8,128)(2,1)S(1)}, u32[]{:S(2)}, u32[]{:S(2)}) collective-permute-start(bf16[256,768]{1,0:T(8,128)(2,1)S(1)} %broadcast_select_fusion.4), channel_id=1, source_target_pairs={{0,4},{4,0},{8,12},{12,8},{16,20},{20,16},{24,28},{28,24},{32,36},... | collective-permute-start | bytes 1179656 | tf_op jit(solution)/shard_map/ppermute | solution.py:45
  117.8 3.9 %collective-permute-start.26 = (bf16[256,768]{1,0:T(8,128)(2,1)S(1)}, bf16[256,768]{1,0:T(8,128)(2,1)S(1)}, u32[]{:S(2)}, u32[]{:S(2)}) collective-permute-start(bf16[256,768]{1,0:T(8,128)(2,1)S(1)} %broadcast_select_fusion.1), channel_id=1, source_target_pairs={{0,4},{4,0},{8,12},{12,8},{16,20},{20,16},{24,28},{28,24},{32,36},... | collective-permute-start | bytes 1179656 | tf_op jit(solution)/shard_map/ppermute | solution.py:45
  122.1 10.5 %collective-permute-start.29 = (bf16[4,64,768]{2,1,0:T(8,128)(2,1)S(1)}, bf16[4,64,768]{2,1,0:T(8,128)(2,1)S(1)}, u32[]{:S(2)}, u32[]{:S(2)}) collective-permute-start(bf16[4,64,768]{2,1,0:T(8,128)(2,1)S(1)} %get-tuple-element.14), channel_id=1, source_target_pairs={{0,64},{4,20},{8,72},{12,28},{16,80},{20,4},{24,88},{28,12},{32,96... | collective-permute-start | bytes 1179656 | tf_op jit(solution)/shard_map/ppermute | solution.py:108
  123.4 9.7 %collective-permute-start.28 = (bf16[4,64,768]{2,1,0:T(8,128)(2,1)S(1)}, bf16[4,64,768]{2,1,0:T(8,128)(2,1)S(1)}, u32[]{:S(2)}, u32[]{:S(2)}) collective-permute-start(bf16[4,64,768]{2,1,0:T(8,128)(2,1)S(1)} %get-tuple-element.15), channel_id=1, source_target_pairs={{0,96},{4,28},{8,104},{12,4},{16,112},{20,12},{24,120},{28,20},{32... | collective-permute-start | bytes 1179656 | tf_op jit(solution)/shard_map/ppermute | solution.py:108
  124.8 10.0 %collective-permute-start.27 = (bf16[4,64,768]{2,1,0:T(8,128)(2,1)S(1)}, bf16[4,64,768]{2,1,0:T(8,128)(2,1)S(1)}, u32[]{:S(2)}, u32[]{:S(2)}) collective-permute-start(bf16[4,64,768]{2,1,0:T(8,128)(2,1)S(1)} %get-tuple-element.13), channel_id=1, source_target_pairs={{0,32},{4,12},{8,40},{12,20},{16,48},{20,28},{24,56},{28,4},{32,64... | collective-permute-start | bytes 1179656 | tf_op jit(solution)/shard_map/ppermute | solution.py:108
  135.1 5.1 %collective-permute-start.36 = (bf16[64,768]{1,0:T(8,128)(2,1)S(1)}, bf16[64,768]{1,0:T(8,128)(2,1)S(1)}, u32[]{:S(2)}, u32[]{:S(2)}) collective-permute-start(bf16[64,768]{1,0:T(8,128)(2,1)S(1)} %get-tuple-element.19), channel_id=1, source_target_pairs={{0,16},{4,68},{8,24},{12,76},{16,0},{20,84},{24,8},{28,92},{32,48}... | collective-permute-start | bytes 294920 | tf_op jit(solution)/shard_map/ppermute | solution.py:108
  135.2 5.0 %collective-permute-start.35 = (bf16[64,768]{1,0:T(8,128)(2,1)S(1)}, bf16[64,768]{1,0:T(8,128)(2,1)S(1)}, u32[]{:S(2)}, u32[]{:S(2)}) collective-permute-start(bf16[64,768]{1,0:T(8,128)(2,1)S(1)} %get-tuple-element.20), channel_id=1, source_target_pairs={{0,24},{4,100},{8,0},{12,108},{16,8},{20,116},{24,16},{28,124},{32... | collective-permute-start | bytes 294920 | tf_op jit(solution)/shard_map/ppermute | solution.py:108
  136.6 5.0 %collective-permute-start.34 = (bf16[64,768]{1,0:T(8,128)(2,1)S(1)}, bf16[64,768]{1,0:T(8,128)(2,1)S(1)}, u32[]{:S(2)}, u32[]{:S(2)}) collective-permute-start(bf16[64,768]{1,0:T(8,128)(2,1)S(1)} %get-tuple-element.18), channel_id=1, source_target_pairs={{0,8},{4,36},{8,16},{12,44},{16,24},{20,52},{24,0},{28,60},{32,40}... | collective-permute-start | bytes 294920 | tf_op jit(solution)/shard_map/ppermute | solution.py:108
  141.6 4.8 %collective-permute-start.37 = (bf16[32,768]{1,0:T(8,128)(2,1)S(1)}, bf16[32,768]{1,0:T(8,128)(2,1)S(1)}, u32[]{:S(2)}, u32[]{:S(2)}) collective-permute-start(bf16[32,768]{1,0:T(8,128)(2,1)S(1)} %get-tuple-element.36), channel_id=1, source_target_pairs={{0,4},{4,0},{8,12},{12,8},{16,20},{20,16},{24,28},{28,24},{32,36},... | collective-permute-start | bytes 147464 | tf_op jit(solution)/shard_map/ppermute | solution.py:45

commit v2 on v1

--- a/solution.py
+++ b/solution.py
@@ -77,7 +77,7 @@
 
 
 def after(v, *done):
-    return lax.optimization_barrier((v,) + done)[0]
+    return lax.optimization_barrier((v, done))[0]
 
 
 def ordered(even, ours, other, axis):
@@ -103,12 +103,12 @@
     return out
 
 
-def line_reduce(v, place, x_core):
+def line_reduce(v, place, x_core, *done):
     pieces = [
         lax.ppermute(take(v, place + shift), "row", plane_step(shift, x_core)) for shift in SHIFTS
     ]
     total = take(v, place).astype(F32)
-    for piece in pieces:
+    for piece in after(pieces, *done):
         total = total + piece.astype(F32)
     return total
 
@@ -132,47 +132,54 @@
     cot = line_join(cot_line, pieces, second)
     cot = jnp.where(even, cot, cot.swapaxes(0, 1)).reshape(-1, cot.shape[-1])
     cot = ordered(even, cot, swap_cores(cot), 1)
+    cot = after(cot, act_below, act_above)
     tokens = cot.reshape(NZ, -1, cot.shape[1])
     slope = after(slope, cot_line)
 
-    pieces = line_send(after(input_line, cot), 1)
-    inputs = line_join(input_line, pieces, second)
-    inputs = jnp.where(even, inputs, inputs.swapaxes(0, 1)).reshape(-1, inputs.shape[-1])
-    inputs = ordered(even, inputs, swap_cores(inputs), 1)
-
     width = down_weight.shape[0] // CHUNKS
+    chunks = range(CHUNKS)
 
     def share(k, shift):
         return dot(take(tokens, z + shift), down_weight[k * width : (k + 1) * width], 1, 1)
 
-    chunks = range(CHUNKS)
-    far = [send_z_by_core(share(k, 2).astype(BF16)) for k in chunks]
-    act_far = send_z_by_core(jnp.where(even, act_below, act_above))
-
+    opposite = [share(k, 2).astype(BF16) for k in chunks]
+    far = [send_z_by_core(v) for v in opposite]
     sides = []
     for k in chunks:
         got = far[k].astype(F32)
         zero = jnp.zeros_like(got)
         up = (share(k, 1) + jnp.where(even, got, zero)).astype(BF16)
         down = (share(k, -1) + jnp.where(even, zero, got)).astype(BF16)
-        sides.append((send_z(up, 1), send_z(down, -1)))
+        sides.append([send_z(up, 1), send_z(down, -1)])
+
     own, near = [], []
     for k in chunks:
+        if k > 0:
+            sides[k] = after(sides[k], own[k - 1])
         total = share(k, 0) + sides[k][0].astype(F32) + sides[k][1].astype(F32)
         own.append((total * slope[:, k * width : (k + 1) * width]).astype(BF16))
-        near.append((send_z(own[k], 1), send_z(own[k], -1)))
-
+        near.append([send_z(own[k], 1), send_z(own[k], -1)])
+
+    input_pieces = line_send(after(input_line, own[-1]), 1)
+
+
+    last = []
+    for k in chunks:
+        if k > 0:
+            near[k] = after(near[k], onward)
+        onward = jnp.where(even, *near[k])
+        last.append(send_z_by_core(onward))
+
+    act_far = send_z_by_core(after(jnp.where(even, act_below, act_above), onward))
     act_all = jnp.zeros((NZ,) + activated.shape, BF16)
     for shift, block in ((0, activated), (-1, act_below), (1, act_above), (2, act_far)):
         act_all = put(act_all, block, z + shift)
     down_grad = dot(act_all.reshape(-1, act_all.shape[2]), cot, 0, 0).astype(BF16)
 
-    last = []
-    for k in chunks:
-        onward = jnp.where(even, *near[k])
-        if k == 0:
-            onward = after(onward, down_grad)
-        last.append(send_z_by_core(onward))
+    last[-1] = after(last[-1], input_pieces)
+    inputs = line_join(input_line, input_pieces, second)
+    inputs = jnp.where(even, inputs, inputs.swapaxes(0, 1)).reshape(-1, inputs.shape[-1])
+    inputs = ordered(even, inputs, swap_cores(inputs), 1)
 
     hidden = jnp.zeros((NZ,) + preact.shape, BF16)
     plane = jnp.zeros((NY,) + (preact.shape[0], up_weight.shape[0] // 2), BF16)
@@ -186,11 +193,12 @@
         hidden = put(hidden, block, z + shift)
         ours, theirs = halves(dot(block, up_weight, 1, 1).astype(BF16), even)
         plane = put(plane, (ours + swap_cores(theirs).astype(F32)).astype(BF16), z + shift)
+    up_grad = dot(inputs, hidden.reshape(-1, hidden.shape[2]), 0, 0).astype(BF16)
 
     plane = plane.reshape(NY, NX, -1, plane.shape[-1])
-    line = line_reduce(jnp.where(even, plane, plane.swapaxes(0, 1)), second, 1).astype(BF16)
-    up_grad = dot(inputs, hidden.reshape(-1, hidden.shape[2]), 0, 0).astype(BF16)
-    pair = line_reduce(after(line, up_grad), first, 0).astype(BF16)
+    plane = jnp.where(even, plane, plane.swapaxes(0, 1))
+    line = line_reduce(plane, second, 1, up_grad).astype(BF16)
+    pair = line_reduce(line, first, 0).astype(BF16)
     n = pair.shape[0] // 2
     upper, lower = pair[:n], pair[n:]
     other = swap_cores(jnp.where(even, lower, upper))

time: 147 us -> 133 us (0.905)
  waiting for transfers between devices: 53.6 us -> 39.4 us
    ppermute x5, waiting for transfers between devices: 16.7 us -> 3.8 us  [send_z_by_core(): return lax.ppermute(v, ('row', 'col'), Z_BY_CORE)]
    ppermute x6, starting transfers between devices: 4.41 us -> 7.47 us  [line_reduce(): lax.ppermute(take(v, place + shift), 'row', plane_step(shift, x_core))]
    ppermute x9, starting transfers between devices: 14.3 us -> 11.8 us  [line_send(): lax.ppermute(v, 'row', plane_step(shift, x_core))]
    ppermute x6, waiting for transfers between devices: 7.05 us -> 5.39 us  [line_reduce(): lax.ppermute(take(v, place + shift), 'row', plane_step(shift, x_core))]
  transfers between devices with their start and end apart: 38 -> 38, of which waited for: 17 -> 19; matrix products, arithmetic and copies ran while one was open for 21% -> 25% of each run, Pallas kernels for 0% -> 0%
where the time goes in v2:
time: 133 us
  starting transfers between devices  56 us (42%)
  waiting for transfers between devices  39.4 us (30%)
  matrix products  26.6 us (20%)
  other arithmetic  7.52 us (6%)
  local copies, waits for them, and re-layouts  1.94 us (1%)
    dot_general x14, matrix products, dot(): lax.dot_general(a, b, (((ca,), (cb,)), ((), ())), preferred_element_type=...  26.6 us
    ppermute x10, waiting for transfers between devices, send_z(): return lax.ppermute(v, 'col', z_step(shift))  18 us
    ppermute x8, starting transfers between devices, swap_cores(): return lax.ppermute(v, 'row', SIBLING)  16.2 us
    ppermute x10, starting transfers between devices, send_z(): return lax.ppermute(v, 'col', z_step(shift))  15.4 us
    ppermute x9, starting transfers between devices, line_send(): lax.ppermute(v, 'row', plane_step(shift, x_core))  11.8 us
    ppermute x9, waiting for transfers between devices, line_send(): lax.ppermute(v, 'row', plane_step(shift, x_core))  7.96 us
    ppermute x6, starting transfers between devices, line_reduce(): lax.ppermute(take(v, place + shift), 'row', plane_step(shift, x_core))  7.47 us
    ppermute x6, waiting for transfers between devices, line_reduce(): lax.ppermute(take(v, place + shift), 'row', plane_step(shift, x_core))  5.39 us
  transfers between devices with their start and end apart: 38, of which 19 were waited for; matrix products, arithmetic and copies ran while one was open for 25% of the time, Pallas kernels for 0%

profile of v2, /device:TPU:1, one launch (start us, length us, event | category | flops | bytes accessed | tf_op | source)
XLA Modules:
  0.0 132.7 jit_solution(4329188002876666516)
XLA Ops:
  0.6 1.0 broadcast_select_fusion.8
  1.6 1.5 %collective-permute-start = (bf16[2,32,768]{2,1,0:T(8,128)(2,1)S(1)}, bf16[2,32,768]{2,1,0:T(8,128)(2,1)S(1)}, u32[]{:S(2)}, u32[]{:S(2)}) collective-permute-start(bf16[2,32,768]{2,1,0:T(8,128)(2,1)S(1)} %get-tuple-element.56), channel_id=1, source_target_pairs={{0,4},{4,0},{8,12},{12,8},{16,20},{20,16},{24,28},{28,24},{32,36},... | collective-permute-start | bytes 294920 | tf_op jit(solution)/shard_map/ppermute | solution.py:45
  3.1 0.9 collective-permute-done
  4.1 1.4 %collective-permute-start.1 = (bf16[2,64,768]{2,1,0:T(8,128)(2,1)S(1)}, bf16[2,64,768]{2,1,0:T(8,128)(2,1)S(1)}, u32[]{:S(2)}, u32[]{:S(2)}) collective-permute-start(bf16[2,64,768]{2,1,0:T(8,128)(2,1)S(1)} %maximum_select_fusion.3), channel_id=1, source_target_pairs={{0,8},{4,36},{8,16},{12,44},{16,24},{20,52},{24,0},{28,60},{32,40}... | collective-permute-start | bytes 589832 | tf_op jit(solution)/shard_map/ppermute | solution.py:96
  5.5 1.5 %collective-permute-start.2 = (bf16[2,64,768]{2,1,0:T(8,128)(2,1)S(1)}, bf16[2,64,768]{2,1,0:T(8,128)(2,1)S(1)}, u32[]{:S(2)}, u32[]{:S(2)}) collective-permute-start(bf16[2,64,768]{2,1,0:T(8,128)(2,1)S(1)} %maximum_select_fusion.3), channel_id=1, source_target_pairs={{0,24},{4,100},{8,0},{12,108},{16,8},{20,116},{24,16},{28,124},{32... | collective-permute-start | bytes 589832 | tf_op jit(solution)/shard_map/ppermute | solution.py:96
  7.1 1.6 %collective-permute-start.3 = (bf16[2,64,768]{2,1,0:T(8,128)(2,1)S(1)}, bf16[2,64,768]{2,1,0:T(8,128)(2,1)S(1)}, u32[]{:S(2)}, u32[]{:S(2)}) collective-permute-start(bf16[2,64,768]{2,1,0:T(8,128)(2,1)S(1)} %maximum_select_fusion.3), channel_id=1, source_target_pairs={{0,16},{4,68},{8,24},{12,76},{16,0},{20,84},{24,8},{28,92},{32,48}... | collective-permute-start | bytes 589832 | tf_op jit(solution)/shard_map/ppermute | solution.py:96
  8.6 2.2 %fusion.8 = (bf16[256,1536]{1,0:T(8,128)(2,1)S(1)}, f32[256,1536]{1,0:T(8,128)S(1)}) fusion(bf16[256,1536]{1,0:T(8,128)(2,1)} %param.7), kind=kLoop, calls=%fused_computation.23 | loop fusion | flops 7864320 | bytes 3145728 | tf_op jit(solution)/shard_map/convert_element_type | solution.py:128
  10.8 1.7 %collective-permute-start.8 = (bf16[256,1536]{1,0:T(8,128)(2,1)S(1)}, bf16[256,1536]{1,0:T(8,128)(2,1)S(1)}, u32[]{:S(2)}, u32[]{:S(2)}) collective-permute-start(bf16[256,1536]{1,0:T(8,128)(2,1)S(1)} %get-tuple-element.38), channel_id=1, source_target_pairs={{0,1},{1,2},{2,3},{3,0},{4,5},{5,6},{6,7},{7,4},{8,9},{9,10},{10,1... | collective-permute-start | bytes 2359304 | tf_op jit(solution)/shard_map/ppermute | solution.py:49
  12.5 2.2 %collective-permute-start.9 = (bf16[256,1536]{1,0:T(8,128)(2,1)S(1)}, bf16[256,1536]{1,0:T(8,128)(2,1)S(1)}, u32[]{:S(2)}, u32[]{:S(2)}) collective-permute-start(bf16[256,1536]{1,0:T(8,128)(2,1)S(1)} %get-tuple-element.38), channel_id=1, source_target_pairs={{0,3},{1,0},{2,1},{3,2},{4,7},{5,4},{6,5},{7,6},{8,11},{9,8},{10,9... | collective-permute-start | bytes 2359304 | tf_op jit(solution)/shard_map/ppermute | solution.py:49
  15.0 1.3 collective-permute-start.4
  17.1 2.0 %collective-permute-start.5 = (bf16[4,64,768]{2,1,0:T(8,128)(2,1)S(1)}, bf16[4,64,768]{2,1,0:T(8,128)(2,1)S(1)}, u32[]{:S(2)}, u32[]{:S(2)}) collective-permute-start(bf16[4,64,768]{2,1,0:T(8,128)(2,1)S(1)} %get-tuple-element.50), channel_id=1, source_target_pairs={{0,96},{4,28},{8,104},{12,4},{16,112},{20,12},{24,120},{28,20},{32... | collective-permute-start | bytes 1179656 | tf_op jit(solution)/shard_map/ppermute | solution.py:96
  19.1 1.1 collective-permute-start.6
  20.3 2.8 %collective-permute-done.4 = bf16[4,64,768]{2,1,0:T(8,128)(2,1)S(1)} collective-permute-done((bf16[4,64,768]{2,1,0:T(8,128)(2,1)S(1)}, bf16[4,64,768]{2,1,0:T(8,128)(2,1)S(1)}, u32[]{:S(2)}, u32[]{:S(2)}) %collective-permute-start.4) | collective-permute-done | bytes 393248 | tf_op jit(solution)/shard_map/ppermute | solution.py:96
  23.2 4.8 %collective-permute-done.5 = bf16[4,64,768]{2,1,0:T(8,128)(2,1)S(1)} collective-permute-done((bf16[4,64,768]{2,1,0:T(8,128)(2,1)S(1)}, bf16[4,64,768]{2,1,0:T(8,128)(2,1)S(1)}, u32[]{:S(2)}, u32[]{:S(2)}) %collective-permute-start.5) | collective-permute-done | bytes 393248 | tf_op jit(solution)/shard_map/ppermute | solution.py:96
  28.5 2.5 %collective-permute-start.7 = (bf16[1024,768]{1,0:T(8,128)(2,1)S(1)}, bf16[1024,768]{1,0:T(8,128)(2,1)S(1)}, u32[]{:S(2)}, u32[]{:S(2)}) collective-permute-start(bf16[1024,768]{1,0:T(8,128)(2,1)S(1)} %bitcast.134), channel_id=1, source_target_pairs={{0,4},{4,0},{8,12},{12,8},{16,20},{20,16},{24,28},{28,24},{32,36},... | collective-permute-start | bytes 4718600 | tf_op jit(solution)/shard_map/ppermute | solution.py:45
  31.7 2.3 %collective-permute-done.7 = bf16[1024,768]{1,0:T(8,128)(2,1)S(1)} collective-permute-done((bf16[1024,768]{1,0:T(8,128)(2,1)S(1)}, bf16[1024,768]{1,0:T(8,128)(2,1)S(1)}, u32[]{:S(2)}, u32[]{:S(2)}) %collective-permute-start.7) | collective-permute-done | bytes 1572896 | tf_op jit(solution)/shard_map/ppermute | solution.py:45
  34.1 0.9 maximum_select_fusion
  35.0 0.8 fusion.31
  35.8 2.6 %collective-permute-start.10 = (bf16[256,768]{1,0:T(8,128)(2,1)S(1)}, bf16[256,768]{1,0:T(8,128)(2,1)S(1)}, u32[]{:S(2)}, u32[]{:S(2)}) collective-permute-start(bf16[256,768]{1,0:T(8,128)(2,1)S(1)} %fusion.31), channel_id=1, source_target_pairs={{0,1},{1,2},{2,3},{3,0},{4,7},{5,4},{6,5},{7,6},{8,9},{9,10},{10,1... | collective-permute-start | bytes 1179656 | tf_op jit(solution)/shard_map/ppermute | solution.py:53
  38.4 0.8 fusion.34
  39.4 0.8 fusion.29
  40.2 2.9 %collective-permute-done.10 = bf16[256,768]{1,0:T(8,128)(2,1)S(1)} collective-permute-done((bf16[256,768]{1,0:T(8,128)(2,1)S(1)}, bf16[256,768]{1,0:T(8,128)(2,1)S(1)}, u32[]{:S(2)}, u32[]{:S(2)}) %collective-permute-start.10) | collective-permute-done | bytes 393248 | tf_op jit(solution)/shard_map/ppermute | solution.py:53
  43.1 0.8 fusion.38
  44.3 0.8 fusion.40
  45.1 2.9 %collective-permute-start.12 = (bf16[256,768]{1,0:T(8,128)(2,1)S(1)}, bf16[256,768]{1,0:T(8,128)(2,1)S(1)}, u32[]{:S(2)}, u32[]{:S(2)}) collective-permute-start(bf16[256,768]{1,0:T(8,128)(2,1)S(1)} %fusion.40), channel_id=1, source_target_pairs={{0,3},{1,0},{2,1},{3,2},{4,7},{5,4},{6,5},{7,6},{8,11},{9,8},{10,9... | collective-permute-start | bytes 1179656 | tf_op jit(solution)/shard_map/ppermute | solution.py:49
  48.0 0.8 fusion.44
  48.8 2.7 %collective-permute-start.15 = (bf16[256,768]{1,0:T(8,128)(2,1)S(1)}, bf16[256,768]{1,0:T(8,128)(2,1)S(1)}, u32[]{:S(2)}, u32[]{:S(2)}) collective-permute-start(bf16[256,768]{1,0:T(8,128)(2,1)S(1)} %fusion.44), channel_id=1, source_target_pairs={{0,3},{1,0},{2,1},{3,2},{4,7},{5,4},{6,5},{7,6},{8,11},{9,8},{10,9... | collective-permute-start | bytes 1179656 | tf_op jit(solution)/shard_map/ppermute | solution.py:49
  51.5 0.8 fusion.42
  52.4 0.8 fusion.21
  53.2 2.7 %collective-permute-done.11 = bf16[256,768]{1,0:T(8,128)(2,1)S(1)} collective-permute-done((bf16[256,768]{1,0:T(8,128)(2,1)S(1)}, bf16[256,768]{1,0:T(8,128)(2,1)S(1)}, u32[]{:S(2)}, u32[]{:S(2)}) %collective-permute-start.11) | collective-permute-done | bytes 393248 | tf_op jit(solution)/shard_map/ppermute | solution.py:49
  56.2 1.4 %collective-permute-start.17 = (bf16[256,768]{1,0:T(8,128)(2,1)S(1)}, bf16[256,768]{1,0:T(8,128)(2,1)S(1)}, u32[]{:S(2)}, u32[]{:S(2)}) collective-permute-start(bf16[256,768]{1,0:T(8,128)(2,1)S(1)} %multiply_convert_fusion.1), channel_id=1, source_target_pairs={{0,1},{1,2},{2,3},{3,0},{4,5},{5,6},{6,7},{7,4},{8,9},{9,10},{10,1... | collective-permute-start | bytes 1179656 | tf_op jit(solution)/shard_map/ppermute | solution.py:49
  57.6 1.3 collective-permute-start.20
  58.9 4.0 %collective-permute-done.15 = bf16[256,768]{1,0:T(8,128)(2,1)S(1)} collective-permute-done((bf16[256,768]{1,0:T(8,128)(2,1)S(1)}, bf16[256,768]{1,0:T(8,128)(2,1)S(1)}, u32[]{:S(2)}, u32[]{:S(2)}) %collective-permute-start.15) | collective-permute-done | bytes 393248 | tf_op jit(solution)/shard_map/ppermute | solution.py:49
  62.9 1.9 %collective-permute-done.14 = bf16[256,768]{1,0:T(8,128)(2,1)S(1)} collective-permute-done((bf16[256,768]{1,0:T(8,128)(2,1)S(1)}, bf16[256,768]{1,0:T(8,128)(2,1)S(1)}, u32[]{:S(2)}, u32[]{:S(2)}) %collective-permute-start.14) | collective-permute-done | bytes 393248 | tf_op jit(solution)/shard_map/ppermute | solution.py:49
  65.0 1.0 collective-permute-start.18
  66.0 1.7 %collective-permute-start.19 = (bf16[256,768]{1,0:T(8,128)(2,1)S(1)}, bf16[256,768]{1,0:T(8,128)(2,1)S(1)}, u32[]{:S(2)}, u32[]{:S(2)}) collective-permute-start(bf16[256,768]{1,0:T(8,128)(2,1)S(1)} %multiply_convert_fusion), channel_id=1, source_target_pairs={{0,3},{1,0},{2,1},{3,2},{4,7},{5,4},{6,5},{7,6},{8,11},{9,8},{10,9... | collective-permute-start | bytes 1179656 | tf_op jit(solution)/shard_map/ppermute | solution.py:49
  68.3 1.4 %convolution_convert_fusion.5 = bf16[256,1536]{1,0:T(8,128)(2,1)S(1)} fusion(bf16[1536,1536]{1,0:T(8,128)(2,1)S(1)} %bitcast.153, bf16[256,768]{1,0:T(8,128)(2,1)S(1)} %multiply_convert_fusion, bf16[256,768]{1,0:T(8,128)(2,1)S(1)} %multiply_convert_fusion.1), kind=kOutput, calls=%fused_computation.20 | convolution fusion | flops 1209925632 | bytes 6291456 | tf_op jit(solution)/shard_map/dot_general | solution.py:57
  70.1 3.1 %collective-permute-done.17 = bf16[256,768]{1,0:T(8,128)(2,1)S(1)} collective-permute-done((bf16[256,768]{1,0:T(8,128)(2,1)S(1)}, bf16[256,768]{1,0:T(8,128)(2,1)S(1)}, u32[]{:S(2)}, u32[]{:S(2)}) %collective-permute-start.17) | collective-permute-done | bytes 393248 | tf_op jit(solution)/shard_map/ppermute | solution.py:49
  73.2 1.4 %collective-permute-start.26 = (bf16[4,64,768]{2,1,0:T(8,128)(2,1)S(1)}, bf16[4,64,768]{2,1,0:T(8,128)(2,1)S(1)}, u32[]{:S(2)}, u32[]{:S(2)}) collective-permute-start(bf16[4,64,768]{2,1,0:T(8,128)(2,1)S(1)} %get-tuple-element.26), channel_id=1, source_target_pairs={{0,96},{4,28},{8,104},{12,4},{16,112},{20,12},{24,120},{28,20},{32... | collective-permute-start | bytes 1179656 | tf_op jit(solution)/shard_map/ppermute | solution.py:96
  74.6 1.0 collective-permute-start.27
  75.7 5.9 %collective-permute-done.18 = bf16[256,768]{1,0:T(8,128)(2,1)S(1)} collective-permute-done((bf16[256,768]{1,0:T(8,128)(2,1)S(1)}, bf16[256,768]{1,0:T(8,128)(2,1)S(1)}, u32[]{:S(2)}, u32[]{:S(2)}) %collective-permute-start.18) | collective-permute-done | bytes 393248 | tf_op jit(solution)/shard_map/ppermute | solution.py:49
  81.7 1.5 %collective-permute-start.16 = (bf16[256,768]{1,0:T(8,128)(2,1)S(1)}, bf16[256,768]{1,0:T(8,128)(2,1)S(1)}, u32[]{:S(2)}, u32[]{:S(2)}) collective-permute-start(bf16[256,768]{1,0:T(8,128)(2,1)S(1)} %broadcast_select_fusion.6), channel_id=1, source_target_pairs={{0,4},{4,0},{8,12},{12,8},{16,20},{20,16},{24,28},{28,24},{32,36},... | collective-permute-start | bytes 1179656 | tf_op jit(solution)/shard_map/ppermute | solution.py:45
  83.3 1.4 %collective-permute-start.24 = (bf16[256,768]{1,0:T(8,128)(2,1)S(1)}, bf16[256,768]{1,0:T(8,128)(2,1)S(1)}, u32[]{:S(2)}, u32[]{:S(2)}) collective-permute-start(bf16[256,768]{1,0:T(8,128)(2,1)S(1)} %get-tuple-element.43), channel_id=1, source_target_pairs={{0,1},{1,2},{2,3},{3,0},{4,7},{5,4},{6,5},{7,6},{8,9},{9,10},{10,1... | collective-permute-start | bytes 1179656 | tf_op jit(solution)/shard_map/ppermute | solution.py:53
  85.1 0.6 collective-permute-start.37
  86.0 3.5 %collective-permute-start.32 = (bf16[1024,768]{1,0:T(8,128)(2,1)S(1)}, bf16[1024,768]{1,0:T(8,128)(2,1)S(1)}, u32[]{:S(2)}, u32[]{:S(2)}) collective-permute-start(bf16[1024,768]{1,0:T(8,128)(2,1)S(1)} %bitcast.146), channel_id=1, source_target_pairs={{0,4},{4,0},{8,12},{12,8},{16,20},{20,16},{24,28},{28,24},{32,36},... | collective-permute-start | bytes 4718600 | tf_op jit(solution)/shard_map/ppermute | solution.py:45
  89.6 1.4 %convolution_convert_fusion.4 = bf16[256,1536]{1,0:T(8,128)(2,1)S(1)} fusion(bf16[256,1536]{1,0:T(8,128)(2,1)S(1)} %get-tuple-element.45, bf16[1536,1536]{1,0:T(8,128)(2,1)S(1)} %bitcast.153), kind=kOutput, calls=%fused_computation.19 | convolution fusion | flops 1208352768 | bytes 6291456 | tf_op jit(solution)/shard_map/dot_general | solution.py:57
  91.0 1.4 %convolution_convert_fusion.3 = bf16[256,1536]{1,0:T(8,128)(2,1)S(1)} fusion(bf16[256,1536]{1,0:T(8,128)(2,1)S(1)} %get-tuple-element.44, bf16[1536,1536]{1,0:T(8,128)(2,1)S(1)} %bitcast.153), kind=kOutput, calls=%fused_computation.18 | convolution fusion | flops 1208352768 | bytes 6291456 | tf_op jit(solution)/shard_map/dot_general | solution.py:57
  93.6 0.9 collective-permute-done.23
  94.5 1.4 %convolution_convert_fusion.2 = bf16[256,1536]{1,0:T(8,128)(2,1)S(1)} fusion(bf16[256,1536]{1,0:T(8,128)(2,1)S(1)} %constant_dynamic-update-slice_fusion.4, bf16[1536,1536]{1,0:T(8,128)(2,1)S(1)} %bitcast.153), kind=kOutput, calls=%fused_computation.17 | convolution fusion | flops 1208352768 | bytes 6291456 | tf_op jit(solution)/shard_map/dot_general | solution.py:57
  96.0 2.4 %collective-permute-start.28 = (bf16[256,768]{1,0:T(8,128)(2,1)S(1)}, bf16[256,768]{1,0:T(8,128)(2,1)S(1)}, u32[]{:S(2)}, u32[]{:S(2)}) collective-permute-start(bf16[256,768]{1,0:T(8,128)(2,1)S(1)} %broadcast_select_fusion.1), channel_id=1, source_target_pairs={{0,4},{4,0},{8,12},{12,8},{16,20},{20,16},{24,28},{28,24},{32,36},... | collective-permute-start | bytes 1179656 | tf_op jit(solution)/shard_map/ppermute | solution.py:45
  98.8 1.0 collective-permute-done.28
  100.2 0.7 collective-permute-start.29
  100.8 2.1 %collective-permute-start.30 = (bf16[4,64,768]{2,1,0:T(8,128)(2,1)S(1)}, bf16[4,64,768]{2,1,0:T(8,128)(2,1)S(1)}, u32[]{:S(2)}, u32[]{:S(2)}) collective-permute-start(bf16[4,64,768]{2,1,0:T(8,128)(2,1)S(1)} %get-tuple-element.36), channel_id=1, source_target_pairs={{0,96},{4,28},{8,104},{12,4},{16,112},{20,12},{24,120},{28,20},{32... | collective-permute-start | bytes 1179656 | tf_op jit(solution)/shard_map/ppermute | solution.py:108
  103.3 7.7 %convolution_convert_fusion.1 = bf16[1536,1536]{1,0:T(8,128)(2,1)} fusion(bf16[1024,1536]{1,0:T(8,128)(2,1)S(1)} %bitcast.145, bf16[1024,768]{1,0:T(8,128)(2,1)S(1)} %collective-permute-done.32, bf16[1024,768]{1,0:T(8,128)(2,1)S(1)} %bitcast.147, pred[]{:T(512)S(6)} %eq.50), kind=kOutput, calls=%fused_computation.1 | convolution fusion | flops 4848353280 | bytes 11010049 | tf_op jit(solution)/shard_map/dot_general | solution.py:57
  111.0 0.9 collective-permute-done.30
  111.8 0.7 collective-permute-done.31
  112.8 1.8 %collective-permute-start.33 = (bf16[64,768]{1,0:T(8,128)(2,1)S(1)}, bf16[64,768]{1,0:T(8,128)(2,1)S(1)}, u32[]{:S(2)}, u32[]{:S(2)}) collective-permute-start(bf16[64,768]{1,0:T(8,128)(2,1)S(1)} %get-tuple-element.42), channel_id=1, source_target_pairs={{0,8},{4,36},{8,16},{12,44},{16,24},{20,52},{24,0},{28,60},{32,40}... | collective-permute-start | bytes 294920 | tf_op jit(solution)/shard_map/ppermute | solution.py:108
  114.6 1.4 %collective-permute-start.34 = (bf16[64,768]{1,0:T(8,128)(2,1)S(1)}, bf16[64,768]{1,0:T(8,128)(2,1)S(1)}, u32[]{:S(2)}, u32[]{:S(2)}) collective-permute-start(bf16[64,768]{1,0:T(8,128)(2,1)S(1)} %get-tuple-element.41), channel_id=1, source_target_pairs={{0,24},{4,100},{8,0},{12,108},{16,8},{20,116},{24,16},{28,124},{32... | collective-permute-start | bytes 294920 | tf_op jit(solution)/shard_map/ppermute | solution.py:108
  116.1 1.1 collective-permute-start.35
  117.2 0.8 collective-permute-done.33
  118.1 2.9 %collective-permute-done.35 = bf16[64,768]{1,0:T(8,128)(2,1)S(1)} collective-permute-done((bf16[64,768]{1,0:T(8,128)(2,1)S(1)}, bf16[64,768]{1,0:T(8,128)(2,1)S(1)}, u32[]{:S(2)}, u32[]{:S(2)}) %collective-permute-start.35) | collective-permute-done | bytes 98336 | tf_op jit(solution)/shard_map/ppermute | solution.py:108
  121.1 4.1 %collective-permute-start.36 = (bf16[32,768]{1,0:T(8,128)(2,1)S(1)}, bf16[32,768]{1,0:T(8,128)(2,1)S(1)}, u32[]{:S(2)}, u32[]{:S(2)}) collective-permute-start(bf16[32,768]{1,0:T(8,128)(2,1)S(1)} %get-tuple-element.58), channel_id=1, source_target_pairs={{0,4},{4,0},{8,12},{12,8},{16,20},{20,16},{24,28},{28,24},{32,36},... | collective-permute-start | bytes 147464 | tf_op jit(solution)/shard_map/ppermute | solution.py:45
  125.2 6.8 %convolution_convert_fusion = bf16[1536,1536]{1,0:T(8,128)(2,1)} fusion(bf16[1024,1536]{1,0:T(8,128)(2,1)S(1)} %bitcast.144, bf16[1024,1536]{1,0:T(8,128)(2,1)S(1)} %maximum_select_fusion), kind=kOutput, calls=%fused_computation | convolution fusion | flops 4834197504 | bytes 11010048 | tf_op jit(solution)/shard_map/dot_general | solution.py:57
  132.0 0.7 maximum_select_fusion.4
  (95 shorter events, 8.1 us)
Async XLA Ops:
  1.6 2.4 %collective-permute-start = (bf16[2,32,768]{2,1,0:T(8,128)(2,1)S(1)}, bf16[2,32,768]{2,1,0:T(8,128)(2,1)S(1)}, u32[]{:S(2)}, u32[]{:S(2)}) collective-permute-start(bf16[2,32,768]{2,1,0:T(8,128)(2,1)S(1)} %get-tuple-element.56), channel_id=1, source_target_pairs={{0,4},{4,0},{8,12},{12,8},{16,20},{20,16},{24,28},{28,24},{32,36},... | collective-permute-start | bytes 294920 | tf_op jit(solution)/shard_map/ppermute | solution.py:45
  4.1 10.7 %collective-permute-start.1 = (bf16[2,64,768]{2,1,0:T(8,128)(2,1)S(1)}, bf16[2,64,768]{2,1,0:T(8,128)(2,1)S(1)}, u32[]{:S(2)}, u32[]{:S(2)}) collective-permute-start(bf16[2,64,768]{2,1,0:T(8,128)(2,1)S(1)} %maximum_select_fusion.3), channel_id=1, source_target_pairs={{0,8},{4,36},{8,16},{12,44},{16,24},{20,52},{24,0},{28,60},{32,40}... | collective-permute-start | bytes 589832 | tf_op jit(solution)/shard_map/ppermute | solution.py:96
  5.5 9.3 %collective-permute-start.2 = (bf16[2,64,768]{2,1,0:T(8,128)(2,1)S(1)}, bf16[2,64,768]{2,1,0:T(8,128)(2,1)S(1)}, u32[]{:S(2)}, u32[]{:S(2)}) collective-permute-start(bf16[2,64,768]{2,1,0:T(8,128)(2,1)S(1)} %maximum_select_fusion.3), channel_id=1, source_target_pairs={{0,24},{4,100},{8,0},{12,108},{16,8},{20,116},{24,16},{28,124},{32... | collective-permute-start | bytes 589832 | tf_op jit(solution)/shard_map/ppermute | solution.py:96
  7.1 7.9 %collective-permute-start.3 = (bf16[2,64,768]{2,1,0:T(8,128)(2,1)S(1)}, bf16[2,64,768]{2,1,0:T(8,128)(2,1)S(1)}, u32[]{:S(2)}, u32[]{:S(2)}) collective-permute-start(bf16[2,64,768]{2,1,0:T(8,128)(2,1)S(1)} %maximum_select_fusion.3), channel_id=1, source_target_pairs={{0,16},{4,68},{8,24},{12,76},{16,0},{20,84},{24,8},{28,92},{32,48}... | collective-permute-start | bytes 589832 | tf_op jit(solution)/shard_map/ppermute | solution.py:96
  10.8 20.7 %collective-permute-start.8 = (bf16[256,1536]{1,0:T(8,128)(2,1)S(1)}, bf16[256,1536]{1,0:T(8,128)(2,1)S(1)}, u32[]{:S(2)}, u32[]{:S(2)}) collective-permute-start(bf16[256,1536]{1,0:T(8,128)(2,1)S(1)} %get-tuple-element.38), channel_id=1, source_target_pairs={{0,1},{1,2},{2,3},{3,0},{4,5},{5,6},{6,7},{7,4},{8,9},{9,10},{10,1... | collective-permute-start | bytes 2359304 | tf_op jit(solution)/shard_map/ppermute | solution.py:49
  12.5 19.0 %collective-permute-start.9 = (bf16[256,1536]{1,0:T(8,128)(2,1)S(1)}, bf16[256,1536]{1,0:T(8,128)(2,1)S(1)}, u32[]{:S(2)}, u32[]{:S(2)}) collective-permute-start(bf16[256,1536]{1,0:T(8,128)(2,1)S(1)} %get-tuple-element.38), channel_id=1, source_target_pairs={{0,3},{1,0},{2,1},{3,2},{4,7},{5,4},{6,5},{7,6},{8,11},{9,8},{10,9... | collective-permute-start | bytes 2359304 | tf_op jit(solution)/shard_map/ppermute | solution.py:49
  14.8 1.7 %copy-start = (bf16[256,1536]{1,0:T(8,128)(2,1)S(1)}, bf16[256,1536]{1,0:T(8,128)(2,1)}, u32[]{:S(2)}) copy-start(bf16[256,1536]{1,0:T(8,128)(2,1)} %param.7) | copy-start | bytes 2359300
  15.0 8.2 %collective-permute-start.4 = (bf16[4,64,768]{2,1,0:T(8,128)(2,1)S(1)}, bf16[4,64,768]{2,1,0:T(8,128)(2,1)S(1)}, u32[]{:S(2)}, u32[]{:S(2)}) collective-permute-start(bf16[4,64,768]{2,1,0:T(8,128)(2,1)S(1)} %get-tuple-element.50), channel_id=1, source_target_pairs={{0,32},{4,12},{8,40},{12,20},{16,48},{20,28},{24,56},{28,4},{32,64... | collective-permute-start | bytes 1179656 | tf_op jit(solution)/shard_map/ppermute | solution.py:96
  17.1 10.9 %collective-permute-start.5 = (bf16[4,64,768]{2,1,0:T(8,128)(2,1)S(1)}, bf16[4,64,768]{2,1,0:T(8,128)(2,1)S(1)}, u32[]{:S(2)}, u32[]{:S(2)}) collective-permute-start(bf16[4,64,768]{2,1,0:T(8,128)(2,1)S(1)} %get-tuple-element.50), channel_id=1, source_target_pairs={{0,96},{4,28},{8,104},{12,4},{16,112},{20,12},{24,120},{28,20},{32... | collective-permute-start | bytes 1179656 | tf_op jit(solution)/shard_map/ppermute | solution.py:96
  19.1 9.3 %collective-permute-start.6 = (bf16[4,64,768]{2,1,0:T(8,128)(2,1)S(1)}, bf16[4,64,768]{2,1,0:T(8,128)(2,1)S(1)}, u32[]{:S(2)}, u32[]{:S(2)}) collective-permute-start(bf16[4,64,768]{2,1,0:T(8,128)(2,1)S(1)} %get-tuple-element.50), channel_id=1, source_target_pairs={{0,64},{4,20},{8,72},{12,28},{16,80},{20,4},{24,88},{28,12},{32,96... | collective-permute-start | bytes 1179656 | tf_op jit(solution)/shard_map/ppermute | solution.py:96
  28.5 5.5 %collective-permute-start.7 = (bf16[1024,768]{1,0:T(8,128)(2,1)S(1)}, bf16[1024,768]{1,0:T(8,128)(2,1)S(1)}, u32[]{:S(2)}, u32[]{:S(2)}) collective-permute-start(bf16[1024,768]{1,0:T(8,128)(2,1)S(1)} %bitcast.134), channel_id=1, source_target_pairs={{0,4},{4,0},{8,12},{12,8},{16,20},{20,16},{24,28},{28,24},{32,36},... | collective-permute-start | bytes 4718600 | tf_op jit(solution)/shard_map/ppermute | solution.py:45
  31.2 3.7 %slice-start = ((s8[4718592]{0:T(1024)(128)(4,1)}), s8[4194304]{0:T(1024)(128)(4,1)S(1)}, s32[]{:S(2)}) async-start(s8[4718592]{0:T(1024)(128)(4,1)} %bitcast.150), calls=%async_computation | async-start | bytes 8388608
  31.6 3.3 %slice-start.1 = ((s8[4718592]{0:T(1024)(128)(4,1)}), s8[524288]{0:T(1024)(128)(4,1)S(1)}, s32[]{:S(2)}) async-start(s8[4718592]{0:T(1024)(128)(4,1)} %bitcast.150), calls=%async_computation.1 | async-start | bytes 1048576
  35.8 7.3 %collective-permute-start.10 = (bf16[256,768]{1,0:T(8,128)(2,1)S(1)}, bf16[256,768]{1,0:T(8,128)(2,1)S(1)}, u32[]{:S(2)}, u32[]{:S(2)}) collective-permute-start(bf16[256,768]{1,0:T(8,128)(2,1)S(1)} %fusion.31), channel_id=1, source_target_pairs={{0,1},{1,2},{2,3},{3,0},{4,7},{5,4},{6,5},{7,6},{8,9},{9,10},{10,1... | collective-permute-start | bytes 1179656 | tf_op jit(solution)/shard_map/ppermute | solution.py:53
  39.2 8.8 %collective-permute-start.13 = (bf16[256,768]{1,0:T(8,128)(2,1)S(1)}, bf16[256,768]{1,0:T(8,128)(2,1)S(1)}, u32[]{:S(2)}, u32[]{:S(2)}) collective-permute-start(bf16[256,768]{1,0:T(8,128)(2,1)S(1)} %fusion.34), channel_id=1, source_target_pairs={{0,1},{1,2},{2,3},{3,0},{4,7},{5,4},{6,5},{7,6},{8,9},{9,10},{10,1... | collective-permute-start | bytes 1179656 | tf_op jit(solution)/shard_map/ppermute | solution.py:53
  43.9 12.0 %collective-permute-start.11 = (bf16[256,768]{1,0:T(8,128)(2,1)S(1)}, bf16[256,768]{1,0:T(8,128)(2,1)S(1)}, u32[]{:S(2)}, u32[]{:S(2)}) collective-permute-start(bf16[256,768]{1,0:T(8,128)(2,1)S(1)} %fusion.38), channel_id=1, source_target_pairs={{0,1},{1,2},{2,3},{3,0},{4,5},{5,6},{6,7},{7,4},{8,9},{9,10},{10,1... | collective-permute-start | bytes 1179656 | tf_op jit(solution)/shard_map/ppermute | solution.py:49
  45.1 10.9 %collective-permute-start.12 = (bf16[256,768]{1,0:T(8,128)(2,1)S(1)}, bf16[256,768]{1,0:T(8,128)(2,1)S(1)}, u32[]{:S(2)}, u32[]{:S(2)}) collective-permute-start(bf16[256,768]{1,0:T(8,128)(2,1)S(1)} %fusion.40), channel_id=1, source_target_pairs={{0,3},{1,0},{2,1},{3,2},{4,7},{5,4},{6,5},{7,6},{8,11},{9,8},{10,9... | collective-permute-start | bytes 1179656 | tf_op jit(solution)/shard_map/ppermute | solution.py:49
  48.8 14.1 %collective-permute-start.15 = (bf16[256,768]{1,0:T(8,128)(2,1)S(1)}, bf16[256,768]{1,0:T(8,128)(2,1)S(1)}, u32[]{:S(2)}, u32[]{:S(2)}) collective-permute-start(bf16[256,768]{1,0:T(8,128)(2,1)S(1)} %fusion.44), channel_id=1, source_target_pairs={{0,3},{1,0},{2,1},{3,2},{4,7},{5,4},{6,5},{7,6},{8,11},{9,8},{10,9... | collective-permute-start | bytes 1179656 | tf_op jit(solution)/shard_map/ppermute | solution.py:49
  51.5 16.8 %slice-start.2 = ((s8[4718592]{0:T(1024)(128)(4,1)}), s8[4194304]{0:T(1024)(128)(4,1)S(1)}, s32[]{:S(2)}) async-start(s8[4718592]{0:T(1024)(128)(4,1)} %bitcast.152), calls=%async_computation.2 | async-start | bytes 8388608
  52.3 16.0 %slice-start.3 = ((s8[4718592]{0:T(1024)(128)(4,1)}), s8[524288]{0:T(1024)(128)(4,1)S(1)}, s32[]{:S(2)}) async-start(s8[4718592]{0:T(1024)(128)(4,1)} %bitcast.152), calls=%async_computation.3 | async-start | bytes 1048576
  52.3 12.5 %collective-permute-start.14 = (bf16[256,768]{1,0:T(8,128)(2,1)S(1)}, bf16[256,768]{1,0:T(8,128)(2,1)S(1)}, u32[]{:S(2)}, u32[]{:S(2)}) collective-permute-start(bf16[256,768]{1,0:T(8,128)(2,1)S(1)} %fusion.42), channel_id=1, source_target_pairs={{0,1},{1,2},{2,3},{3,0},{4,5},{5,6},{6,7},{7,4},{8,9},{9,10},{10,1... | collective-permute-start | bytes 1179656 | tf_op jit(solution)/shard_map/ppermute | solution.py:49
  56.2 17.1 %collective-permute-start.17 = (bf16[256,768]{1,0:T(8,128)(2,1)S(1)}, bf16[256,768]{1,0:T(8,128)(2,1)S(1)}, u32[]{:S(2)}, u32[]{:S(2)}) collective-permute-start(bf16[256,768]{1,0:T(8,128)(2,1)S(1)} %multiply_convert_fusion.1), channel_id=1, source_target_pairs={{0,1},{1,2},{2,3},{3,0},{4,5},{5,6},{6,7},{7,4},{8,9},{9,10},{10,1... | collective-permute-start | bytes 1179656 | tf_op jit(solution)/shard_map/ppermute | solution.py:49
  57.6 17.0 %collective-permute-start.20 = (bf16[256,768]{1,0:T(8,128)(2,1)S(1)}, bf16[256,768]{1,0:T(8,128)(2,1)S(1)}, u32[]{:S(2)}, u32[]{:S(2)}) collective-permute-start(bf16[256,768]{1,0:T(8,128)(2,1)S(1)} %multiply_convert_fusion.1), channel_id=1, source_target_pairs={{0,3},{1,0},{2,1},{3,2},{4,7},{5,4},{6,5},{7,6},{8,11},{9,8},{10,9... | collective-permute-start | bytes 1179656 | tf_op jit(solution)/shard_map/ppermute | solution.py:49
  65.0 16.7 %collective-permute-start.18 = (bf16[256,768]{1,0:T(8,128)(2,1)S(1)}, bf16[256,768]{1,0:T(8,128)(2,1)S(1)}, u32[]{:S(2)}, u32[]{:S(2)}) collective-permute-start(bf16[256,768]{1,0:T(8,128)(2,1)S(1)} %multiply_convert_fusion), channel_id=1, source_target_pairs={{0,1},{1,2},{2,3},{3,0},{4,5},{5,6},{6,7},{7,4},{8,9},{9,10},{10,1... | collective-permute-start | bytes 1179656 | tf_op jit(solution)/shard_map/ppermute | solution.py:49
  66.0 17.1 %collective-permute-start.19 = (bf16[256,768]{1,0:T(8,128)(2,1)S(1)}, bf16[256,768]{1,0:T(8,128)(2,1)S(1)}, u32[]{:S(2)}, u32[]{:S(2)}) collective-permute-start(bf16[256,768]{1,0:T(8,128)(2,1)S(1)} %multiply_convert_fusion), channel_id=1, source_target_pairs={{0,3},{1,0},{2,1},{3,2},{4,7},{5,4},{6,5},{7,6},{8,11},{9,8},{10,9... | collective-permute-start | bytes 1179656 | tf_op jit(solution)/shard_map/ppermute | solution.py:49
  67.7 16.9 %collective-permute-start.25 = (bf16[4,64,768]{2,1,0:T(8,128)(2,1)S(1)}, bf16[4,64,768]{2,1,0:T(8,128)(2,1)S(1)}, u32[]{:S(2)}, u32[]{:S(2)}) collective-permute-start(bf16[4,64,768]{2,1,0:T(8,128)(2,1)S(1)} %get-tuple-element.26), channel_id=1, source_target_pairs={{0,32},{4,12},{8,40},{12,20},{16,48},{20,28},{24,56},{28,4},{32,64... | collective-permute-start | bytes 1179656 | tf_op jit(solution)/shard_map/ppermute | solution.py:96
  73.2 11.8 %collective-permute-start.26 = (bf16[4,64,768]{2,1,0:T(8,128)(2,1)S(1)}, bf16[4,64,768]{2,1,0:T(8,128)(2,1)S(1)}, u32[]{:S(2)}, u32[]{:S(2)}) collective-permute-start(bf16[4,64,768]{2,1,0:T(8,128)(2,1)S(1)} %get-tuple-element.26), channel_id=1, source_target_pairs={{0,96},{4,28},{8,104},{12,4},{16,112},{20,12},{24,120},{28,20},{32... | collective-permute-start | bytes 1179656 | tf_op jit(solution)/shard_map/ppermute | solution.py:96
  74.6 11.1 %collective-permute-start.27 = (bf16[4,64,768]{2,1,0:T(8,128)(2,1)S(1)}, bf16[4,64,768]{2,1,0:T(8,128)(2,1)S(1)}, u32[]{:S(2)}, u32[]{:S(2)}) collective-permute-start(bf16[4,64,768]{2,1,0:T(8,128)(2,1)S(1)} %get-tuple-element.26), channel_id=1, source_target_pairs={{0,64},{4,20},{8,72},{12,28},{16,80},{20,4},{24,88},{28,12},{32,96... | collective-permute-start | bytes 1179656 | tf_op jit(solution)/shard_map/ppermute | solution.py:96
  81.7 10.9 %collective-permute-start.16 = (bf16[256,768]{1,0:T(8,128)(2,1)S(1)}, bf16[256,768]{1,0:T(8,128)(2,1)S(1)}, u32[]{:S(2)}, u32[]{:S(2)}) collective-permute-start(bf16[256,768]{1,0:T(8,128)(2,1)S(1)} %broadcast_select_fusion.6), channel_id=1, source_target_pairs={{0,4},{4,0},{8,12},{12,8},{16,20},{20,16},{24,28},{28,24},{32,36},... | collective-permute-start | bytes 1179656 | tf_op jit(solution)/shard_map/ppermute | solution.py:45
  83.3 9.7 %collective-permute-start.24 = (bf16[256,768]{1,0:T(8,128)(2,1)S(1)}, bf16[256,768]{1,0:T(8,128)(2,1)S(1)}, u32[]{:S(2)}, u32[]{:S(2)}) collective-permute-start(bf16[256,768]{1,0:T(8,128)(2,1)S(1)} %get-tuple-element.43), channel_id=1, source_target_pairs={{0,1},{1,2},{2,3},{3,0},{4,7},{5,4},{6,5},{7,6},{8,9},{9,10},{10,1... | collective-permute-start | bytes 1179656 | tf_op jit(solution)/shard_map/ppermute | solution.py:53
  84.7 9.8 %collective-permute-start.23 = (bf16[256,768]{1,0:T(8,128)(2,1)S(1)}, bf16[256,768]{1,0:T(8,128)(2,1)S(1)}, u32[]{:S(2)}, u32[]{:S(2)}) collective-permute-start(bf16[256,768]{1,0:T(8,128)(2,1)S(1)} %get-tuple-element.47), channel_id=1, source_target_pairs={{0,1},{1,2},{2,3},{3,0},{4,7},{5,4},{6,5},{7,6},{8,9},{9,10},{10,1... | collective-permute-start | bytes 1179656 | tf_op jit(solution)/shard_map/ppermute | solution.py:53
  85.1 32.1 %collective-permute-start.37 = (bf16[256,1536]{1,0:T(8,128)(2,1)S(1)}, bf16[256,1536]{1,0:T(8,128)(2,1)S(1)}, u32[]{:S(2)}, u32[]{:S(2)}) collective-permute-start(bf16[256,1536]{1,0:T(8,128)(2,1)S(1)} %broadcast_select_fusion), channel_id=1, source_target_pairs={{0,1},{1,2},{2,3},{3,0},{4,7},{5,4},{6,5},{7,6},{8,9},{9,10},{10,1... | collective-permute-start | bytes 2359304 | tf_op jit(solution)/shard_map/ppermute | solution.py:53
  86.0 17.2 %collective-permute-start.32 = (bf16[1024,768]{1,0:T(8,128)(2,1)S(1)}, bf16[1024,768]{1,0:T(8,128)(2,1)S(1)}, u32[]{:S(2)}, u32[]{:S(2)}) collective-permute-start(bf16[1024,768]{1,0:T(8,128)(2,1)S(1)} %bitcast.146), channel_id=1, source_target_pairs={{0,4},{4,0},{8,12},{12,8},{16,20},{20,16},{24,28},{28,24},{32,36},... | collective-permute-start | bytes 4718600 | tf_op jit(solution)/shard_map/ppermute | solution.py:45
  92.6 5.8 %collective-permute-start.21 = (bf16[256,768]{1,0:T(8,128)(2,1)S(1)}, bf16[256,768]{1,0:T(8,128)(2,1)S(1)}, u32[]{:S(2)}, u32[]{:S(2)}) collective-permute-start(bf16[256,768]{1,0:T(8,128)(2,1)S(1)} %broadcast_select_fusion.4), channel_id=1, source_target_pairs={{0,4},{4,0},{8,12},{12,8},{16,20},{20,16},{24,28},{28,24},{32,36},... | collective-permute-start | bytes 1179656 | tf_op jit(solution)/shard_map/ppermute | solution.py:45
  93.0 5.5 %collective-permute-start.22 = (bf16[256,768]{1,0:T(8,128)(2,1)S(1)}, bf16[256,768]{1,0:T(8,128)(2,1)S(1)}, u32[]{:S(2)}, u32[]{:S(2)}) collective-permute-start(bf16[256,768]{1,0:T(8,128)(2,1)S(1)} %broadcast_select_fusion.3), channel_id=1, source_target_pairs={{0,4},{4,0},{8,12},{12,8},{16,20},{20,16},{24,28},{28,24},{32,36},... | collective-permute-start | bytes 1179656 | tf_op jit(solution)/shard_map/ppermute | solution.py:45
  96.0 3.7 %collective-permute-start.28 = (bf16[256,768]{1,0:T(8,128)(2,1)S(1)}, bf16[256,768]{1,0:T(8,128)(2,1)S(1)}, u32[]{:S(2)}, u32[]{:S(2)}) collective-permute-start(bf16[256,768]{1,0:T(8,128)(2,1)S(1)} %broadcast_select_fusion.1), channel_id=1, source_target_pairs={{0,4},{4,0},{8,12},{12,8},{16,20},{20,16},{24,28},{28,24},{32,36},... | collective-permute-start | bytes 1179656 | tf_op jit(solution)/shard_map/ppermute | solution.py:45
  100.2 10.8 %collective-permute-start.29 = (bf16[4,64,768]{2,1,0:T(8,128)(2,1)S(1)}, bf16[4,64,768]{2,1,0:T(8,128)(2,1)S(1)}, u32[]{:S(2)}, u32[]{:S(2)}) collective-permute-start(bf16[4,64,768]{2,1,0:T(8,128)(2,1)S(1)} %get-tuple-element.37), channel_id=1, source_target_pairs={{0,32},{4,12},{8,40},{12,20},{16,48},{20,28},{24,56},{28,4},{32,64... | collective-permute-start | bytes 1179656 | tf_op jit(solution)/shard_map/ppermute | solution.py:108
  100.8 11.0 %collective-permute-start.30 = (bf16[4,64,768]{2,1,0:T(8,128)(2,1)S(1)}, bf16[4,64,768]{2,1,0:T(8,128)(2,1)S(1)}, u32[]{:S(2)}, u32[]{:S(2)}) collective-permute-start(bf16[4,64,768]{2,1,0:T(8,128)(2,1)S(1)} %get-tuple-element.36), channel_id=1, source_target_pairs={{0,96},{4,28},{8,104},{12,4},{16,112},{20,12},{24,120},{28,20},{32... | collective-permute-start | bytes 1179656 | tf_op jit(solution)/shard_map/ppermute | solution.py:108
  102.9 9.7 %collective-permute-start.31 = (bf16[4,64,768]{2,1,0:T(8,128)(2,1)S(1)}, bf16[4,64,768]{2,1,0:T(8,128)(2,1)S(1)}, u32[]{:S(2)}, u32[]{:S(2)}) collective-permute-start(bf16[4,64,768]{2,1,0:T(8,128)(2,1)S(1)} %get-tuple-element.35), channel_id=1, source_target_pairs={{0,64},{4,20},{8,72},{12,28},{16,80},{20,4},{24,88},{28,12},{32,96... | collective-permute-start | bytes 1179656 | tf_op jit(solution)/shard_map/ppermute | solution.py:108
  112.8 5.2 %collective-permute-start.33 = (bf16[64,768]{1,0:T(8,128)(2,1)S(1)}, bf16[64,768]{1,0:T(8,128)(2,1)S(1)}, u32[]{:S(2)}, u32[]{:S(2)}) collective-permute-start(bf16[64,768]{1,0:T(8,128)(2,1)S(1)} %get-tuple-element.42), channel_id=1, source_target_pairs={{0,8},{4,36},{8,16},{12,44},{16,24},{20,52},{24,0},{28,60},{32,40}... | collective-permute-start | bytes 294920 | tf_op jit(solution)/shard_map/ppermute | solution.py:108
  114.6 3.5 %collective-permute-start.34 = (bf16[64,768]{1,0:T(8,128)(2,1)S(1)}, bf16[64,768]{1,0:T(8,128)(2,1)S(1)}, u32[]{:S(2)}, u32[]{:S(2)}) collective-permute-start(bf16[64,768]{1,0:T(8,128)(2,1)S(1)} %get-tuple-element.41), channel_id=1, source_target_pairs={{0,24},{4,100},{8,0},{12,108},{16,8},{20,116},{24,16},{28,124},{32... | collective-permute-start | bytes 294920 | tf_op jit(solution)/shard_map/ppermute | solution.py:108
  116.1 5.0 %collective-permute-start.35 = (bf16[64,768]{1,0:T(8,128)(2,1)S(1)}, bf16[64,768]{1,0:T(8,128)(2,1)S(1)}, u32[]{:S(2)}, u32[]{:S(2)}) collective-permute-start(bf16[64,768]{1,0:T(8,128)(2,1)S(1)} %get-tuple-element.40), channel_id=1, source_target_pairs={{0,16},{4,68},{8,24},{12,76},{16,0},{20,84},{24,8},{28,92},{32,48}... | collective-permute-start | bytes 294920 | tf_op jit(solution)/shard_map/ppermute | solution.py:108
  121.1 10.9 %collective-permute-start.36 = (bf16[32,768]{1,0:T(8,128)(2,1)S(1)}, bf16[32,768]{1,0:T(8,128)(2,1)S(1)}, u32[]{:S(2)}, u32[]{:S(2)}) collective-permute-start(bf16[32,768]{1,0:T(8,128)(2,1)S(1)} %get-tuple-element.58), channel_id=1, source_target_pairs={{0,4},{4,0},{8,12},{12,8},{16,20},{20,16},{24,28},{28,24},{32,36},... | collective-permute-start | bytes 147464 | tf_op jit(solution)/shard_map/ppermute | solution.py:45

commit v3 on v2

--- a/solution.py
+++ b/solution.py
@@ -9,7 +9,7 @@
 F32 = jnp.float32
 NY, NX, NZ = 4, 4, 4
 CHUNKS = 2
-SHIFTS = (1, -1, 2)
+SHIFTS = (2, 1, -1)
 
 
 def device(y, x, core):

time: 133 us -> 130 us (0.977)
  starting transfers between devices: 56 us -> 54.6 us
    ppermute x9, starting transfers between devices: 11.8 us -> 14.4 us  [line_send(): lax.ppermute(v, 'row', plane_step(shift, x_core))]
    ppermute x8, starting transfers between devices: 16.2 us -> 13.9 us  [swap_cores(): return lax.ppermute(v, 'row', SIBLING)]
    ppermute x9, waiting for transfers between devices: 7.96 us -> 6.14 us  [line_send(): lax.ppermute(v, 'row', plane_step(shift, x_core))]
    ppermute x5, waiting for transfers between devices: 3.8 us -> 5.61 us  [send_z_by_core(): return lax.ppermute(v, ('row', 'col'), Z_BY_CORE)]
    ppermute x5, starting transfers between devices: 5.15 us -> 3.38 us  [send_z_by_core(): return lax.ppermute(v, ('row', 'col'), Z_BY_CORE)]
    ppermute x6, waiting for transfers between devices: 5.39 us -> 4.05 us  [line_reduce(): lax.ppermute(take(v, place + shift), 'row', plane_step(shift, x_core))]
  transfers between devices with their start and end apart: 38 -> 38, of which waited for: 19 -> 17; matrix products, arithmetic and copies ran while one was open for 25% -> 25% of each run, Pallas kernels for 0% -> 0%
where the time goes in v3:
time: 130 us
  starting transfers between devices  54.6 us (42%)
  waiting for transfers between devices  38.3 us (29%)
  matrix products  26.6 us (20%)
  other arithmetic  7.52 us (6%)
  local copies, waits for them, and re-layouts  1.94 us (1%)
    dot_general x14, matrix products, dot(): lax.dot_general(a, b, (((ca,), (cb,)), ((), ())), preferred_element_type=...  26.6 us
    ppermute x10, waiting for transfers between devices, send_z(): return lax.ppermute(v, 'col', z_step(shift))  18.8 us
    ppermute x10, starting transfers between devices, send_z(): return lax.ppermute(v, 'col', z_step(shift))  14.9 us
    ppermute x9, starting transfers between devices, line_send(): lax.ppermute(v, 'row', plane_step(shift, x_core))  14.4 us
    ppermute x8, starting transfers between devices, swap_cores(): return lax.ppermute(v, 'row', SIBLING)  13.9 us
    ppermute x6, starting transfers between devices, line_reduce(): lax.ppermute(take(v, place + shift), 'row', plane_step(shift, x_core))  8.06 us
    ppermute x9, waiting for transfers between devices, line_send(): lax.ppermute(v, 'row', plane_step(shift, x_core))  6.14 us
    ppermute x5, waiting for transfers between devices, send_z_by_core(): return lax.ppermute(v, ('row', 'col'), Z_BY_CORE)  5.61 us
  transfers between devices with their start and end apart: 38, of which 17 were waited for; matrix products, arithmetic and copies ran while one was open for 25% of the time, Pallas kernels for 0%

profile of v3, /device:TPU:1, one launch (start us, length us, event | category | flops | bytes accessed | tf_op | source)
XLA Modules:
  0.0 130.2 jit_solution(106892510076918548)
XLA Ops:
  0.6 1.0 broadcast_select_fusion.8
  1.6 1.5 %collective-permute-start = (bf16[2,32,768]{2,1,0:T(8,128)(2,1)S(1)}, bf16[2,32,768]{2,1,0:T(8,128)(2,1)S(1)}, u32[]{:S(2)}, u32[]{:S(2)}) collective-permute-start(bf16[2,32,768]{2,1,0:T(8,128)(2,1)S(1)} %get-tuple-element.56), channel_id=1, source_target_pairs={{0,4},{4,0},{8,12},{12,8},{16,20},{20,16},{24,28},{28,24},{32,36},... | collective-permute-start | bytes 294920 | tf_op jit(solution)/shard_map/ppermute | solution.py:45
  3.1 0.9 collective-permute-done
  4.1 3.1 %collective-permute-start.1 = (bf16[2,64,768]{2,1,0:T(8,128)(2,1)S(1)}, bf16[2,64,768]{2,1,0:T(8,128)(2,1)S(1)}, u32[]{:S(2)}, u32[]{:S(2)}) collective-permute-start(bf16[2,64,768]{2,1,0:T(8,128)(2,1)S(1)} %maximum_select_fusion.3), channel_id=1, source_target_pairs={{0,16},{4,68},{8,24},{12,76},{16,0},{20,84},{24,8},{28,92},{32,48}... | collective-permute-start | bytes 589832 | tf_op jit(solution)/shard_map/ppermute | solution.py:96
  7.2 0.4 collective-permute-start.2
  7.6 2.3 %collective-permute-start.3 = (bf16[2,64,768]{2,1,0:T(8,128)(2,1)S(1)}, bf16[2,64,768]{2,1,0:T(8,128)(2,1)S(1)}, u32[]{:S(2)}, u32[]{:S(2)}) collective-permute-start(bf16[2,64,768]{2,1,0:T(8,128)(2,1)S(1)} %maximum_select_fusion.3), channel_id=1, source_target_pairs={{0,24},{4,100},{8,0},{12,108},{16,8},{20,116},{24,16},{28,124},{32... | collective-permute-start | bytes 589832 | tf_op jit(solution)/shard_map/ppermute | solution.py:96
  9.8 2.2 %fusion.8 = (bf16[256,1536]{1,0:T(8,128)(2,1)S(1)}, f32[256,1536]{1,0:T(8,128)S(1)}) fusion(bf16[256,1536]{1,0:T(8,128)(2,1)} %param.7), kind=kLoop, calls=%fused_computation.23 | loop fusion | flops 7864320 | bytes 3145728 | tf_op jit(solution)/shard_map/convert_element_type | solution.py:128
  12.0 1.7 %collective-permute-start.8 = (bf16[256,1536]{1,0:T(8,128)(2,1)S(1)}, bf16[256,1536]{1,0:T(8,128)(2,1)S(1)}, u32[]{:S(2)}, u32[]{:S(2)}) collective-permute-start(bf16[256,1536]{1,0:T(8,128)(2,1)S(1)} %get-tuple-element.38), channel_id=1, source_target_pairs={{0,1},{1,2},{2,3},{3,0},{4,5},{5,6},{6,7},{7,4},{8,9},{9,10},{10,1... | collective-permute-start | bytes 2359304 | tf_op jit(solution)/shard_map/ppermute | solution.py:49
  13.7 2.2 %collective-permute-start.9 = (bf16[256,1536]{1,0:T(8,128)(2,1)S(1)}, bf16[256,1536]{1,0:T(8,128)(2,1)S(1)}, u32[]{:S(2)}, u32[]{:S(2)}) collective-permute-start(bf16[256,1536]{1,0:T(8,128)(2,1)S(1)} %get-tuple-element.38), channel_id=1, source_target_pairs={{0,3},{1,0},{2,1},{3,2},{4,7},{5,4},{6,5},{7,6},{8,11},{9,8},{10,9... | collective-permute-start | bytes 2359304 | tf_op jit(solution)/shard_map/ppermute | solution.py:49
  16.2 2.8 %collective-permute-start.4 = (bf16[4,64,768]{2,1,0:T(8,128)(2,1)S(1)}, bf16[4,64,768]{2,1,0:T(8,128)(2,1)S(1)}, u32[]{:S(2)}, u32[]{:S(2)}) collective-permute-start(bf16[4,64,768]{2,1,0:T(8,128)(2,1)S(1)} %get-tuple-element.50), channel_id=1, source_target_pairs={{0,64},{4,20},{8,72},{12,28},{16,80},{20,4},{24,88},{28,12},{32,96... | collective-permute-start | bytes 1179656 | tf_op jit(solution)/shard_map/ppermute | solution.py:96
  19.3 0.6 bitcast_dynamic-update-slice_fusion.3
  19.8 0.4 collective-permute-start.5
  20.2 2.4 %collective-permute-start.6 = (bf16[4,64,768]{2,1,0:T(8,128)(2,1)S(1)}, bf16[4,64,768]{2,1,0:T(8,128)(2,1)S(1)}, u32[]{:S(2)}, u32[]{:S(2)}) collective-permute-start(bf16[4,64,768]{2,1,0:T(8,128)(2,1)S(1)} %get-tuple-element.50), channel_id=1, source_target_pairs={{0,96},{4,28},{8,104},{12,4},{16,112},{20,12},{24,120},{28,20},{32... | collective-permute-start | bytes 1179656 | tf_op jit(solution)/shard_map/ppermute | solution.py:96
  22.8 1.9 %collective-permute-done.4 = bf16[4,64,768]{2,1,0:T(8,128)(2,1)S(1)} collective-permute-done((bf16[4,64,768]{2,1,0:T(8,128)(2,1)S(1)}, bf16[4,64,768]{2,1,0:T(8,128)(2,1)S(1)}, u32[]{:S(2)}, u32[]{:S(2)}) %collective-permute-start.4) | collective-permute-done | bytes 393248 | tf_op jit(solution)/shard_map/ppermute | solution.py:96
  24.7 4.2 %collective-permute-done.5 = bf16[4,64,768]{2,1,0:T(8,128)(2,1)S(1)} collective-permute-done((bf16[4,64,768]{2,1,0:T(8,128)(2,1)S(1)}, bf16[4,64,768]{2,1,0:T(8,128)(2,1)S(1)}, u32[]{:S(2)}, u32[]{:S(2)}) %collective-permute-start.5) | collective-permute-done | bytes 393248 | tf_op jit(solution)/shard_map/ppermute | solution.py:96
  29.2 2.5 %collective-permute-start.7 = (bf16[1024,768]{1,0:T(8,128)(2,1)S(1)}, bf16[1024,768]{1,0:T(8,128)(2,1)S(1)}, u32[]{:S(2)}, u32[]{:S(2)}) collective-permute-start(bf16[1024,768]{1,0:T(8,128)(2,1)S(1)} %bitcast.134), channel_id=1, source_target_pairs={{0,4},{4,0},{8,12},{12,8},{16,20},{20,16},{24,28},{28,24},{32,36},... | collective-permute-start | bytes 4718600 | tf_op jit(solution)/shard_map/ppermute | solution.py:45
  31.9 0.8 collective-permute-done.8
  33.0 1.7 %collective-permute-done.7 = bf16[1024,768]{1,0:T(8,128)(2,1)S(1)} collective-permute-done((bf16[1024,768]{1,0:T(8,128)(2,1)S(1)}, bf16[1024,768]{1,0:T(8,128)(2,1)S(1)}, u32[]{:S(2)}, u32[]{:S(2)}) %collective-permute-start.7) | collective-permute-done | bytes 1572896 | tf_op jit(solution)/shard_map/ppermute | solution.py:45
  34.7 0.9 maximum_select_fusion
  35.6 0.8 fusion.31
  36.4 1.7 %collective-permute-start.10 = (bf16[256,768]{1,0:T(8,128)(2,1)S(1)}, bf16[256,768]{1,0:T(8,128)(2,1)S(1)}, u32[]{:S(2)}, u32[]{:S(2)}) collective-permute-start(bf16[256,768]{1,0:T(8,128)(2,1)S(1)} %fusion.31), channel_id=1, source_target_pairs={{0,1},{1,2},{2,3},{3,0},{4,7},{5,4},{6,5},{7,6},{8,9},{9,10},{10,1... | collective-permute-start | bytes 1179656 | tf_op jit(solution)/shard_map/ppermute | solution.py:53
  38.1 0.8 fusion.34
  39.1 0.8 fusion.29
  40.0 3.5 %collective-permute-done.10 = bf16[256,768]{1,0:T(8,128)(2,1)S(1)} collective-permute-done((bf16[256,768]{1,0:T(8,128)(2,1)S(1)}, bf16[256,768]{1,0:T(8,128)(2,1)S(1)}, u32[]{:S(2)}, u32[]{:S(2)}) %collective-permute-start.10) | collective-permute-done | bytes 393248 | tf_op jit(solution)/shard_map/ppermute | solution.py:53
  43.4 0.8 fusion.38
  44.3 0.8 fusion.40
  45.1 2.7 %collective-permute-start.12 = (bf16[256,768]{1,0:T(8,128)(2,1)S(1)}, bf16[256,768]{1,0:T(8,128)(2,1)S(1)}, u32[]{:S(2)}, u32[]{:S(2)}) collective-permute-start(bf16[256,768]{1,0:T(8,128)(2,1)S(1)} %fusion.40), channel_id=1, source_target_pairs={{0,3},{1,0},{2,1},{3,2},{4,7},{5,4},{6,5},{7,6},{8,11},{9,8},{10,9... | collective-permute-start | bytes 1179656 | tf_op jit(solution)/shard_map/ppermute | solution.py:49
  47.8 0.8 fusion.44
  48.7 2.6 %collective-permute-start.15 = (bf16[256,768]{1,0:T(8,128)(2,1)S(1)}, bf16[256,768]{1,0:T(8,128)(2,1)S(1)}, u32[]{:S(2)}, u32[]{:S(2)}) collective-permute-start(bf16[256,768]{1,0:T(8,128)(2,1)S(1)} %fusion.44), channel_id=1, source_target_pairs={{0,3},{1,0},{2,1},{3,2},{4,7},{5,4},{6,5},{7,6},{8,11},{9,8},{10,9... | collective-permute-start | bytes 1179656 | tf_op jit(solution)/shard_map/ppermute | solution.py:49
  51.3 0.8 fusion.42
  52.2 0.8 fusion.21
  53.0 3.6 %collective-permute-done.11 = bf16[256,768]{1,0:T(8,128)(2,1)S(1)} collective-permute-done((bf16[256,768]{1,0:T(8,128)(2,1)S(1)}, bf16[256,768]{1,0:T(8,128)(2,1)S(1)}, u32[]{:S(2)}, u32[]{:S(2)}) %collective-permute-start.11) | collective-permute-done | bytes 393248 | tf_op jit(solution)/shard_map/ppermute | solution.py:49
  56.9 2.7 %collective-permute-start.20 = (bf16[256,768]{1,0:T(8,128)(2,1)S(1)}, bf16[256,768]{1,0:T(8,128)(2,1)S(1)}, u32[]{:S(2)}, u32[]{:S(2)}) collective-permute-start(bf16[256,768]{1,0:T(8,128)(2,1)S(1)} %multiply_convert_fusion.1), channel_id=1, source_target_pairs={{0,3},{1,0},{2,1},{3,2},{4,7},{5,4},{6,5},{7,6},{8,11},{9,8},{10,9... | collective-permute-start | bytes 1179656 | tf_op jit(solution)/shard_map/ppermute | solution.py:49
  59.5 2.4 %collective-permute-done.15 = bf16[256,768]{1,0:T(8,128)(2,1)S(1)} collective-permute-done((bf16[256,768]{1,0:T(8,128)(2,1)S(1)}, bf16[256,768]{1,0:T(8,128)(2,1)S(1)}, u32[]{:S(2)}, u32[]{:S(2)}) %collective-permute-start.15) | collective-permute-done | bytes 393248 | tf_op jit(solution)/shard_map/ppermute | solution.py:49
  61.9 3.1 %collective-permute-done.14 = bf16[256,768]{1,0:T(8,128)(2,1)S(1)} collective-permute-done((bf16[256,768]{1,0:T(8,128)(2,1)S(1)}, bf16[256,768]{1,0:T(8,128)(2,1)S(1)}, u32[]{:S(2)}, u32[]{:S(2)}) %collective-permute-start.14) | collective-permute-done | bytes 393248 | tf_op jit(solution)/shard_map/ppermute | solution.py:49
  65.3 2.7 %collective-permute-start.19 = (bf16[256,768]{1,0:T(8,128)(2,1)S(1)}, bf16[256,768]{1,0:T(8,128)(2,1)S(1)}, u32[]{:S(2)}, u32[]{:S(2)}) collective-permute-start(bf16[256,768]{1,0:T(8,128)(2,1)S(1)} %multiply_convert_fusion), channel_id=1, source_target_pairs={{0,3},{1,0},{2,1},{3,2},{4,7},{5,4},{6,5},{7,6},{8,11},{9,8},{10,9... | collective-permute-start | bytes 1179656 | tf_op jit(solution)/shard_map/ppermute | solution.py:49
  67.9 0.4 collective-permute-start.25
  68.4 1.4 %convolution_convert_fusion.5 = bf16[256,1536]{1,0:T(8,128)(2,1)S(1)} fusion(bf16[1536,1536]{1,0:T(8,128)(2,1)S(1)} %bitcast.153, bf16[256,768]{1,0:T(8,128)(2,1)S(1)} %multiply_convert_fusion, bf16[256,768]{1,0:T(8,128)(2,1)S(1)} %multiply_convert_fusion.1), kind=kOutput, calls=%fused_computation.20 | convolution fusion | flops 1209925632 | bytes 6291456 | tf_op jit(solution)/shard_map/dot_general | solution.py:57
  70.2 3.3 %collective-permute-done.17 = bf16[256,768]{1,0:T(8,128)(2,1)S(1)} collective-permute-done((bf16[256,768]{1,0:T(8,128)(2,1)S(1)}, bf16[256,768]{1,0:T(8,128)(2,1)S(1)}, u32[]{:S(2)}, u32[]{:S(2)}) %collective-permute-start.17) | collective-permute-done | bytes 393248 | tf_op jit(solution)/shard_map/ppermute | solution.py:49
  73.4 0.3 collective-permute-start.26
  73.7 2.4 %collective-permute-start.27 = (bf16[4,64,768]{2,1,0:T(8,128)(2,1)S(1)}, bf16[4,64,768]{2,1,0:T(8,128)(2,1)S(1)}, u32[]{:S(2)}, u32[]{:S(2)}) collective-permute-start(bf16[4,64,768]{2,1,0:T(8,128)(2,1)S(1)} %get-tuple-element.26), channel_id=1, source_target_pairs={{0,96},{4,28},{8,104},{12,4},{16,112},{20,12},{24,120},{28,20},{32... | collective-permute-start | bytes 1179656 | tf_op jit(solution)/shard_map/ppermute | solution.py:96
  76.2 5.6 %collective-permute-done.18 = bf16[256,768]{1,0:T(8,128)(2,1)S(1)} collective-permute-done((bf16[256,768]{1,0:T(8,128)(2,1)S(1)}, bf16[256,768]{1,0:T(8,128)(2,1)S(1)}, u32[]{:S(2)}, u32[]{:S(2)}) %collective-permute-start.18) | collective-permute-done | bytes 393248 | tf_op jit(solution)/shard_map/ppermute | solution.py:49
  81.9 1.9 %collective-permute-start.16 = (bf16[256,768]{1,0:T(8,128)(2,1)S(1)}, bf16[256,768]{1,0:T(8,128)(2,1)S(1)}, u32[]{:S(2)}, u32[]{:S(2)}) collective-permute-start(bf16[256,768]{1,0:T(8,128)(2,1)S(1)} %broadcast_select_fusion.6), channel_id=1, source_target_pairs={{0,4},{4,0},{8,12},{12,8},{16,20},{20,16},{24,28},{28,24},{32,36},... | collective-permute-start | bytes 1179656 | tf_op jit(solution)/shard_map/ppermute | solution.py:45
  83.9 1.1 collective-permute-start.24
  85.8 2.5 %collective-permute-start.32 = (bf16[1024,768]{1,0:T(8,128)(2,1)S(1)}, bf16[1024,768]{1,0:T(8,128)(2,1)S(1)}, u32[]{:S(2)}, u32[]{:S(2)}) collective-permute-start(bf16[1024,768]{1,0:T(8,128)(2,1)S(1)} %bitcast.146), channel_id=1, source_target_pairs={{0,4},{4,0},{8,12},{12,8},{16,20},{20,16},{24,28},{28,24},{32,36},... | collective-permute-start | bytes 4718600 | tf_op jit(solution)/shard_map/ppermute | solution.py:45
  88.3 1.4 %convolution_convert_fusion.4 = bf16[256,1536]{1,0:T(8,128)(2,1)S(1)} fusion(bf16[256,1536]{1,0:T(8,128)(2,1)S(1)} %get-tuple-element.45, bf16[1536,1536]{1,0:T(8,128)(2,1)S(1)} %bitcast.153), kind=kOutput, calls=%fused_computation.19 | convolution fusion | flops 1208352768 | bytes 6291456 | tf_op jit(solution)/shard_map/dot_general | solution.py:57
  89.8 1.4 %convolution_convert_fusion.3 = bf16[256,1536]{1,0:T(8,128)(2,1)S(1)} fusion(bf16[256,1536]{1,0:T(8,128)(2,1)S(1)} %get-tuple-element.44, bf16[1536,1536]{1,0:T(8,128)(2,1)S(1)} %bitcast.153), kind=kOutput, calls=%fused_computation.18 | convolution fusion | flops 1208352768 | bytes 6291456 | tf_op jit(solution)/shard_map/dot_general | solution.py:57
  91.8 1.2 collective-permute-start.22
  93.0 2.1 %collective-permute-done.23 = bf16[256,768]{1,0:T(8,128)(2,1)S(1)} collective-permute-done((bf16[256,768]{1,0:T(8,128)(2,1)S(1)}, bf16[256,768]{1,0:T(8,128)(2,1)S(1)}, u32[]{:S(2)}, u32[]{:S(2)}) %collective-permute-start.23) | collective-permute-done | bytes 393248 | tf_op jit(solution)/shard_map/ppermute | solution.py:53
  95.2 1.4 %convolution_convert_fusion.2 = bf16[256,1536]{1,0:T(8,128)(2,1)S(1)} fusion(bf16[256,1536]{1,0:T(8,128)(2,1)S(1)} %constant_dynamic-update-slice_fusion.4, bf16[1536,1536]{1,0:T(8,128)(2,1)S(1)} %bitcast.153), kind=kOutput, calls=%fused_computation.17 | convolution fusion | flops 1208352768 | bytes 6291456 | tf_op jit(solution)/shard_map/dot_general | solution.py:57
  96.6 2.4 %collective-permute-start.28 = (bf16[256,768]{1,0:T(8,128)(2,1)S(1)}, bf16[256,768]{1,0:T(8,128)(2,1)S(1)}, u32[]{:S(2)}, u32[]{:S(2)}) collective-permute-start(bf16[256,768]{1,0:T(8,128)(2,1)S(1)} %broadcast_select_fusion.1), channel_id=1, source_target_pairs={{0,4},{4,0},{8,12},{12,8},{16,20},{20,16},{24,28},{28,24},{32,36},... | collective-permute-start | bytes 1179656 | tf_op jit(solution)/shard_map/ppermute | solution.py:45
  99.4 1.0 collective-permute-done.28
  100.8 0.5 collective-permute-start.29
  101.3 1.3 %collective-permute-start.30 = (bf16[4,64,768]{2,1,0:T(8,128)(2,1)S(1)}, bf16[4,64,768]{2,1,0:T(8,128)(2,1)S(1)}, u32[]{:S(2)}, u32[]{:S(2)}) collective-permute-start(bf16[4,64,768]{2,1,0:T(8,128)(2,1)S(1)} %get-tuple-element.36), channel_id=1, source_target_pairs={{0,32},{4,12},{8,40},{12,20},{16,48},{20,28},{24,56},{28,4},{32,64... | collective-permute-start | bytes 1179656 | tf_op jit(solution)/shard_map/ppermute | solution.py:108
  102.6 1.4 %collective-permute-start.31 = (bf16[4,64,768]{2,1,0:T(8,128)(2,1)S(1)}, bf16[4,64,768]{2,1,0:T(8,128)(2,1)S(1)}, u32[]{:S(2)}, u32[]{:S(2)}) collective-permute-start(bf16[4,64,768]{2,1,0:T(8,128)(2,1)S(1)} %get-tuple-element.35), channel_id=1, source_target_pairs={{0,96},{4,28},{8,104},{12,4},{16,112},{20,12},{24,120},{28,20},{32... | collective-permute-start | bytes 1179656 | tf_op jit(solution)/shard_map/ppermute | solution.py:108
  104.0 7.7 %convolution_convert_fusion.1 = bf16[1536,1536]{1,0:T(8,128)(2,1)} fusion(bf16[1024,1536]{1,0:T(8,128)(2,1)S(1)} %bitcast.145, bf16[1024,768]{1,0:T(8,128)(2,1)S(1)} %collective-permute-done.32, bf16[1024,768]{1,0:T(8,128)(2,1)S(1)} %bitcast.147, pred[]{:T(512)S(6)} %eq.50), kind=kOutput, calls=%fused_computation.1 | convolution fusion | flops 4848353280 | bytes 11010049 | tf_op jit(solution)/shard_map/dot_general | solution.py:57
  111.7 1.8 %collective-permute-done.30 = bf16[4,64,768]{2,1,0:T(8,128)(2,1)S(1)} collective-permute-done((bf16[4,64,768]{2,1,0:T(8,128)(2,1)S(1)}, bf16[4,64,768]{2,1,0:T(8,128)(2,1)S(1)}, u32[]{:S(2)}, u32[]{:S(2)}) %collective-permute-start.30) | collective-permute-done | bytes 393248 | tf_op jit(solution)/shard_map/ppermute | solution.py:108
  113.7 2.2 %collective-permute-start.33 = (bf16[64,768]{1,0:T(8,128)(2,1)S(1)}, bf16[64,768]{1,0:T(8,128)(2,1)S(1)}, u32[]{:S(2)}, u32[]{:S(2)}) collective-permute-start(bf16[64,768]{1,0:T(8,128)(2,1)S(1)} %get-tuple-element.42), channel_id=1, source_target_pairs={{0,16},{4,68},{8,24},{12,76},{16,0},{20,84},{24,8},{28,92},{32,48}... | collective-permute-start | bytes 294920 | tf_op jit(solution)/shard_map/ppermute | solution.py:108
  115.9 0.6 collective-permute-start.34
  116.6 2.0 %collective-permute-start.35 = (bf16[64,768]{1,0:T(8,128)(2,1)S(1)}, bf16[64,768]{1,0:T(8,128)(2,1)S(1)}, u32[]{:S(2)}, u32[]{:S(2)}) collective-permute-start(bf16[64,768]{1,0:T(8,128)(2,1)S(1)} %get-tuple-element.40), channel_id=1, source_target_pairs={{0,24},{4,100},{8,0},{12,108},{16,8},{20,116},{24,16},{28,124},{32... | collective-permute-start | bytes 294920 | tf_op jit(solution)/shard_map/ppermute | solution.py:108
  118.8 2.1 %collective-permute-done.34 = bf16[64,768]{1,0:T(8,128)(2,1)S(1)} collective-permute-done((bf16[64,768]{1,0:T(8,128)(2,1)S(1)}, bf16[64,768]{1,0:T(8,128)(2,1)S(1)}, u32[]{:S(2)}, u32[]{:S(2)}) %collective-permute-start.34) | collective-permute-done | bytes 98336 | tf_op jit(solution)/shard_map/ppermute | solution.py:108
  121.0 1.8 %collective-permute-start.36 = (bf16[32,768]{1,0:T(8,128)(2,1)S(1)}, bf16[32,768]{1,0:T(8,128)(2,1)S(1)}, u32[]{:S(2)}, u32[]{:S(2)}) collective-permute-start(bf16[32,768]{1,0:T(8,128)(2,1)S(1)} %get-tuple-element.58), channel_id=1, source_target_pairs={{0,4},{4,0},{8,12},{12,8},{16,20},{20,16},{24,28},{28,24},{32,36},... | collective-permute-start | bytes 147464 | tf_op jit(solution)/shard_map/ppermute | solution.py:45
  122.8 6.8 %convolution_convert_fusion = bf16[1536,1536]{1,0:T(8,128)(2,1)} fusion(bf16[1024,1536]{1,0:T(8,128)(2,1)S(1)} %bitcast.144, bf16[1024,1536]{1,0:T(8,128)(2,1)S(1)} %maximum_select_fusion), kind=kOutput, calls=%fused_computation | convolution fusion | flops 4834197504 | bytes 11010048 | tf_op jit(solution)/shard_map/dot_general | solution.py:57
  129.6 0.7 maximum_select_fusion.4
  (95 shorter events, 5.4 us)
Async XLA Ops:
  1.6 2.4 %collective-permute-start = (bf16[2,32,768]{2,1,0:T(8,128)(2,1)S(1)}, bf16[2,32,768]{2,1,0:T(8,128)(2,1)S(1)}, u32[]{:S(2)}, u32[]{:S(2)}) collective-permute-start(bf16[2,32,768]{2,1,0:T(8,128)(2,1)S(1)} %get-tuple-element.56), channel_id=1, source_target_pairs={{0,4},{4,0},{8,12},{12,8},{16,20},{20,16},{24,28},{28,24},{32,36},... | collective-permute-start | bytes 294920 | tf_op jit(solution)/shard_map/ppermute | solution.py:45
  4.1 12.0 %collective-permute-start.1 = (bf16[2,64,768]{2,1,0:T(8,128)(2,1)S(1)}, bf16[2,64,768]{2,1,0:T(8,128)(2,1)S(1)}, u32[]{:S(2)}, u32[]{:S(2)}) collective-permute-start(bf16[2,64,768]{2,1,0:T(8,128)(2,1)S(1)} %maximum_select_fusion.3), channel_id=1, source_target_pairs={{0,16},{4,68},{8,24},{12,76},{16,0},{20,84},{24,8},{28,92},{32,48}... | collective-permute-start | bytes 589832 | tf_op jit(solution)/shard_map/ppermute | solution.py:96
  7.2 8.9 %collective-permute-start.2 = (bf16[2,64,768]{2,1,0:T(8,128)(2,1)S(1)}, bf16[2,64,768]{2,1,0:T(8,128)(2,1)S(1)}, u32[]{:S(2)}, u32[]{:S(2)}) collective-permute-start(bf16[2,64,768]{2,1,0:T(8,128)(2,1)S(1)} %maximum_select_fusion.3), channel_id=1, source_target_pairs={{0,8},{4,36},{8,16},{12,44},{16,24},{20,52},{24,0},{28,60},{32,40}... | collective-permute-start | bytes 589832 | tf_op jit(solution)/shard_map/ppermute | solution.py:96
  7.6 8.6 %collective-permute-start.3 = (bf16[2,64,768]{2,1,0:T(8,128)(2,1)S(1)}, bf16[2,64,768]{2,1,0:T(8,128)(2,1)S(1)}, u32[]{:S(2)}, u32[]{:S(2)}) collective-permute-start(bf16[2,64,768]{2,1,0:T(8,128)(2,1)S(1)} %maximum_select_fusion.3), channel_id=1, source_target_pairs={{0,24},{4,100},{8,0},{12,108},{16,8},{20,116},{24,16},{28,124},{32... | collective-permute-start | bytes 589832 | tf_op jit(solution)/shard_map/ppermute | solution.py:96
  12.0 20.7 %collective-permute-start.8 = (bf16[256,1536]{1,0:T(8,128)(2,1)S(1)}, bf16[256,1536]{1,0:T(8,128)(2,1)S(1)}, u32[]{:S(2)}, u32[]{:S(2)}) collective-permute-start(bf16[256,1536]{1,0:T(8,128)(2,1)S(1)} %get-tuple-element.38), channel_id=1, source_target_pairs={{0,1},{1,2},{2,3},{3,0},{4,5},{5,6},{6,7},{7,4},{8,9},{9,10},{10,1... | collective-permute-start | bytes 2359304 | tf_op jit(solution)/shard_map/ppermute | solution.py:49
  13.7 19.1 %collective-permute-start.9 = (bf16[256,1536]{1,0:T(8,128)(2,1)S(1)}, bf16[256,1536]{1,0:T(8,128)(2,1)S(1)}, u32[]{:S(2)}, u32[]{:S(2)}) collective-permute-start(bf16[256,1536]{1,0:T(8,128)(2,1)S(1)} %get-tuple-element.38), channel_id=1, source_target_pairs={{0,3},{1,0},{2,1},{3,2},{4,7},{5,4},{6,5},{7,6},{8,11},{9,8},{10,9... | collective-permute-start | bytes 2359304 | tf_op jit(solution)/shard_map/ppermute | solution.py:49
  16.0 3.2 %copy-start = (bf16[256,1536]{1,0:T(8,128)(2,1)S(1)}, bf16[256,1536]{1,0:T(8,128)(2,1)}, u32[]{:S(2)}) copy-start(bf16[256,1536]{1,0:T(8,128)(2,1)} %param.7) | copy-start | bytes 2359300
  16.2 8.5 %collective-permute-start.4 = (bf16[4,64,768]{2,1,0:T(8,128)(2,1)S(1)}, bf16[4,64,768]{2,1,0:T(8,128)(2,1)S(1)}, u32[]{:S(2)}, u32[]{:S(2)}) collective-permute-start(bf16[4,64,768]{2,1,0:T(8,128)(2,1)S(1)} %get-tuple-element.50), channel_id=1, source_target_pairs={{0,64},{4,20},{8,72},{12,28},{16,80},{20,4},{24,88},{28,12},{32,96... | collective-permute-start | bytes 1179656 | tf_op jit(solution)/shard_map/ppermute | solution.py:96
  19.8 9.1 %collective-permute-start.5 = (bf16[4,64,768]{2,1,0:T(8,128)(2,1)S(1)}, bf16[4,64,768]{2,1,0:T(8,128)(2,1)S(1)}, u32[]{:S(2)}, u32[]{:S(2)}) collective-permute-start(bf16[4,64,768]{2,1,0:T(8,128)(2,1)S(1)} %get-tuple-element.50), channel_id=1, source_target_pairs={{0,32},{4,12},{8,40},{12,20},{16,48},{20,28},{24,56},{28,4},{32,64... | collective-permute-start | bytes 1179656 | tf_op jit(solution)/shard_map/ppermute | solution.py:96
  20.2 8.8 %collective-permute-start.6 = (bf16[4,64,768]{2,1,0:T(8,128)(2,1)S(1)}, bf16[4,64,768]{2,1,0:T(8,128)(2,1)S(1)}, u32[]{:S(2)}, u32[]{:S(2)}) collective-permute-start(bf16[4,64,768]{2,1,0:T(8,128)(2,1)S(1)} %get-tuple-element.50), channel_id=1, source_target_pairs={{0,96},{4,28},{8,104},{12,4},{16,112},{20,12},{24,120},{28,20},{32... | collective-permute-start | bytes 1179656 | tf_op jit(solution)/shard_map/ppermute | solution.py:96
  29.2 5.5 %collective-permute-start.7 = (bf16[1024,768]{1,0:T(8,128)(2,1)S(1)}, bf16[1024,768]{1,0:T(8,128)(2,1)S(1)}, u32[]{:S(2)}, u32[]{:S(2)}) collective-permute-start(bf16[1024,768]{1,0:T(8,128)(2,1)S(1)} %bitcast.134), channel_id=1, source_target_pairs={{0,4},{4,0},{8,12},{12,8},{16,20},{20,16},{24,28},{28,24},{32,36},... | collective-permute-start | bytes 4718600 | tf_op jit(solution)/shard_map/ppermute | solution.py:45
  31.8 3.7 %slice-start = ((s8[4718592]{0:T(1024)(128)(4,1)}), s8[4194304]{0:T(1024)(128)(4,1)S(1)}, s32[]{:S(2)}) async-start(s8[4718592]{0:T(1024)(128)(4,1)} %bitcast.150), calls=%async_computation | async-start | bytes 8388608
  32.9 2.7 %slice-start.1 = ((s8[4718592]{0:T(1024)(128)(4,1)}), s8[524288]{0:T(1024)(128)(4,1)S(1)}, s32[]{:S(2)}) async-start(s8[4718592]{0:T(1024)(128)(4,1)} %bitcast.150), calls=%async_computation.1 | async-start | bytes 1048576
  36.4 7.0 %collective-permute-start.10 = (bf16[256,768]{1,0:T(8,128)(2,1)S(1)}, bf16[256,768]{1,0:T(8,128)(2,1)S(1)}, u32[]{:S(2)}, u32[]{:S(2)}) collective-permute-start(bf16[256,768]{1,0:T(8,128)(2,1)S(1)} %fusion.31), channel_id=1, source_target_pairs={{0,1},{1,2},{2,3},{3,0},{4,7},{5,4},{6,5},{7,6},{8,9},{9,10},{10,1... | collective-permute-start | bytes 1179656 | tf_op jit(solution)/shard_map/ppermute | solution.py:53
  38.9 8.9 %collective-permute-start.13 = (bf16[256,768]{1,0:T(8,128)(2,1)S(1)}, bf16[256,768]{1,0:T(8,128)(2,1)S(1)}, u32[]{:S(2)}, u32[]{:S(2)}) collective-permute-start(bf16[256,768]{1,0:T(8,128)(2,1)S(1)} %fusion.34), channel_id=1, source_target_pairs={{0,1},{1,2},{2,3},{3,0},{4,7},{5,4},{6,5},{7,6},{8,9},{9,10},{10,1... | collective-permute-start | bytes 1179656 | tf_op jit(solution)/shard_map/ppermute | solution.py:53
  44.2 12.4 %collective-permute-start.11 = (bf16[256,768]{1,0:T(8,128)(2,1)S(1)}, bf16[256,768]{1,0:T(8,128)(2,1)S(1)}, u32[]{:S(2)}, u32[]{:S(2)}) collective-permute-start(bf16[256,768]{1,0:T(8,128)(2,1)S(1)} %fusion.38), channel_id=1, source_target_pairs={{0,1},{1,2},{2,3},{3,0},{4,5},{5,6},{6,7},{7,4},{8,9},{9,10},{10,1... | collective-permute-start | bytes 1179656 | tf_op jit(solution)/shard_map/ppermute | solution.py:49
  45.1 11.5 %collective-permute-start.12 = (bf16[256,768]{1,0:T(8,128)(2,1)S(1)}, bf16[256,768]{1,0:T(8,128)(2,1)S(1)}, u32[]{:S(2)}, u32[]{:S(2)}) collective-permute-start(bf16[256,768]{1,0:T(8,128)(2,1)S(1)} %fusion.40), channel_id=1, source_target_pairs={{0,3},{1,0},{2,1},{3,2},{4,7},{5,4},{6,5},{7,6},{8,11},{9,8},{10,9... | collective-permute-start | bytes 1179656 | tf_op jit(solution)/shard_map/ppermute | solution.py:49
  48.7 13.3 %collective-permute-start.15 = (bf16[256,768]{1,0:T(8,128)(2,1)S(1)}, bf16[256,768]{1,0:T(8,128)(2,1)S(1)}, u32[]{:S(2)}, u32[]{:S(2)}) collective-permute-start(bf16[256,768]{1,0:T(8,128)(2,1)S(1)} %fusion.44), channel_id=1, source_target_pairs={{0,3},{1,0},{2,1},{3,2},{4,7},{5,4},{6,5},{7,6},{8,11},{9,8},{10,9... | collective-permute-start | bytes 1179656 | tf_op jit(solution)/shard_map/ppermute | solution.py:49
  51.3 17.1 %slice-start.2 = ((s8[4718592]{0:T(1024)(128)(4,1)}), s8[4194304]{0:T(1024)(128)(4,1)S(1)}, s32[]{:S(2)}) async-start(s8[4718592]{0:T(1024)(128)(4,1)} %bitcast.152), calls=%async_computation.2 | async-start | bytes 8388608
  52.1 16.3 %slice-start.3 = ((s8[4718592]{0:T(1024)(128)(4,1)}), s8[524288]{0:T(1024)(128)(4,1)S(1)}, s32[]{:S(2)}) async-start(s8[4718592]{0:T(1024)(128)(4,1)} %bitcast.152), calls=%async_computation.3 | async-start | bytes 1048576
  52.1 12.9 %collective-permute-start.14 = (bf16[256,768]{1,0:T(8,128)(2,1)S(1)}, bf16[256,768]{1,0:T(8,128)(2,1)S(1)}, u32[]{:S(2)}, u32[]{:S(2)}) collective-permute-start(bf16[256,768]{1,0:T(8,128)(2,1)S(1)} %fusion.42), channel_id=1, source_target_pairs={{0,1},{1,2},{2,3},{3,0},{4,5},{5,6},{6,7},{7,4},{8,9},{9,10},{10,1... | collective-permute-start | bytes 1179656 | tf_op jit(solution)/shard_map/ppermute | solution.py:49
  56.8 16.7 %collective-permute-start.17 = (bf16[256,768]{1,0:T(8,128)(2,1)S(1)}, bf16[256,768]{1,0:T(8,128)(2,1)S(1)}, u32[]{:S(2)}, u32[]{:S(2)}) collective-permute-start(bf16[256,768]{1,0:T(8,128)(2,1)S(1)} %multiply_convert_fusion.1), channel_id=1, source_target_pairs={{0,1},{1,2},{2,3},{3,0},{4,5},{5,6},{6,7},{7,4},{8,9},{9,10},{10,1... | collective-permute-start | bytes 1179656 | tf_op jit(solution)/shard_map/ppermute | solution.py:49
  56.9 16.8 %collective-permute-start.20 = (bf16[256,768]{1,0:T(8,128)(2,1)S(1)}, bf16[256,768]{1,0:T(8,128)(2,1)S(1)}, u32[]{:S(2)}, u32[]{:S(2)}) collective-permute-start(bf16[256,768]{1,0:T(8,128)(2,1)S(1)} %multiply_convert_fusion.1), channel_id=1, source_target_pairs={{0,3},{1,0},{2,1},{3,2},{4,7},{5,4},{6,5},{7,6},{8,11},{9,8},{10,9... | collective-permute-start | bytes 1179656 | tf_op jit(solution)/shard_map/ppermute | solution.py:49
  65.2 16.7 %collective-permute-start.18 = (bf16[256,768]{1,0:T(8,128)(2,1)S(1)}, bf16[256,768]{1,0:T(8,128)(2,1)S(1)}, u32[]{:S(2)}, u32[]{:S(2)}) collective-permute-start(bf16[256,768]{1,0:T(8,128)(2,1)S(1)} %multiply_convert_fusion), channel_id=1, source_target_pairs={{0,1},{1,2},{2,3},{3,0},{4,5},{5,6},{6,7},{7,4},{8,9},{9,10},{10,1... | collective-permute-start | bytes 1179656 | tf_op jit(solution)/shard_map/ppermute | solution.py:49
  65.3 18.5 %collective-permute-start.19 = (bf16[256,768]{1,0:T(8,128)(2,1)S(1)}, bf16[256,768]{1,0:T(8,128)(2,1)S(1)}, u32[]{:S(2)}, u32[]{:S(2)}) collective-permute-start(bf16[256,768]{1,0:T(8,128)(2,1)S(1)} %multiply_convert_fusion), channel_id=1, source_target_pairs={{0,3},{1,0},{2,1},{3,2},{4,7},{5,4},{6,5},{7,6},{8,11},{9,8},{10,9... | collective-permute-start | bytes 1179656 | tf_op jit(solution)/shard_map/ppermute | solution.py:49
  67.9 17.1 %collective-permute-start.25 = (bf16[4,64,768]{2,1,0:T(8,128)(2,1)S(1)}, bf16[4,64,768]{2,1,0:T(8,128)(2,1)S(1)}, u32[]{:S(2)}, u32[]{:S(2)}) collective-permute-start(bf16[4,64,768]{2,1,0:T(8,128)(2,1)S(1)} %get-tuple-element.26), channel_id=1, source_target_pairs={{0,64},{4,20},{8,72},{12,28},{16,80},{20,4},{24,88},{28,12},{32,96... | collective-permute-start | bytes 1179656 | tf_op jit(solution)/shard_map/ppermute | solution.py:96
  73.4 11.8 %collective-permute-start.26 = (bf16[4,64,768]{2,1,0:T(8,128)(2,1)S(1)}, bf16[4,64,768]{2,1,0:T(8,128)(2,1)S(1)}, u32[]{:S(2)}, u32[]{:S(2)}) collective-permute-start(bf16[4,64,768]{2,1,0:T(8,128)(2,1)S(1)} %get-tuple-element.26), channel_id=1, source_target_pairs={{0,32},{4,12},{8,40},{12,20},{16,48},{20,28},{24,56},{28,4},{32,64... | collective-permute-start | bytes 1179656 | tf_op jit(solution)/shard_map/ppermute | solution.py:96
  73.7 11.7 %collective-permute-start.27 = (bf16[4,64,768]{2,1,0:T(8,128)(2,1)S(1)}, bf16[4,64,768]{2,1,0:T(8,128)(2,1)S(1)}, u32[]{:S(2)}, u32[]{:S(2)}) collective-permute-start(bf16[4,64,768]{2,1,0:T(8,128)(2,1)S(1)} %get-tuple-element.26), channel_id=1, source_target_pairs={{0,96},{4,28},{8,104},{12,4},{16,112},{20,12},{24,120},{28,20},{32... | collective-permute-start | bytes 1179656 | tf_op jit(solution)/shard_map/ppermute | solution.py:96
  81.9 9.5 %collective-permute-start.16 = (bf16[256,768]{1,0:T(8,128)(2,1)S(1)}, bf16[256,768]{1,0:T(8,128)(2,1)S(1)}, u32[]{:S(2)}, u32[]{:S(2)}) collective-permute-start(bf16[256,768]{1,0:T(8,128)(2,1)S(1)} %broadcast_select_fusion.6), channel_id=1, source_target_pairs={{0,4},{4,0},{8,12},{12,8},{16,20},{20,16},{24,28},{28,24},{32,36},... | collective-permute-start | bytes 1179656 | tf_op jit(solution)/shard_map/ppermute | solution.py:45
  83.9 7.9 %collective-permute-start.24 = (bf16[256,768]{1,0:T(8,128)(2,1)S(1)}, bf16[256,768]{1,0:T(8,128)(2,1)S(1)}, u32[]{:S(2)}, u32[]{:S(2)}) collective-permute-start(bf16[256,768]{1,0:T(8,128)(2,1)S(1)} %get-tuple-element.43), channel_id=1, source_target_pairs={{0,1},{1,2},{2,3},{3,0},{4,7},{5,4},{6,5},{7,6},{8,9},{9,10},{10,1... | collective-permute-start | bytes 1179656 | tf_op jit(solution)/shard_map/ppermute | solution.py:53
  85.0 10.1 %collective-permute-start.23 = (bf16[256,768]{1,0:T(8,128)(2,1)S(1)}, bf16[256,768]{1,0:T(8,128)(2,1)S(1)}, u32[]{:S(2)}, u32[]{:S(2)}) collective-permute-start(bf16[256,768]{1,0:T(8,128)(2,1)S(1)} %get-tuple-element.47), channel_id=1, source_target_pairs={{0,1},{1,2},{2,3},{3,0},{4,7},{5,4},{6,5},{7,6},{8,9},{9,10},{10,1... | collective-permute-start | bytes 1179656 | tf_op jit(solution)/shard_map/ppermute | solution.py:53
  85.2 33.4 %collective-permute-start.37 = (bf16[256,1536]{1,0:T(8,128)(2,1)S(1)}, bf16[256,1536]{1,0:T(8,128)(2,1)S(1)}, u32[]{:S(2)}, u32[]{:S(2)}) collective-permute-start(bf16[256,1536]{1,0:T(8,128)(2,1)S(1)} %broadcast_select_fusion), channel_id=1, source_target_pairs={{0,1},{1,2},{2,3},{3,0},{4,7},{5,4},{6,5},{7,6},{8,9},{9,10},{10,1... | collective-permute-start | bytes 2359304 | tf_op jit(solution)/shard_map/ppermute | solution.py:53
  85.8 18.2 %collective-permute-start.32 = (bf16[1024,768]{1,0:T(8,128)(2,1)S(1)}, bf16[1024,768]{1,0:T(8,128)(2,1)S(1)}, u32[]{:S(2)}, u32[]{:S(2)}) collective-permute-start(bf16[1024,768]{1,0:T(8,128)(2,1)S(1)} %bitcast.146), channel_id=1, source_target_pairs={{0,4},{4,0},{8,12},{12,8},{16,20},{20,16},{24,28},{28,24},{32,36},... | collective-permute-start | bytes 4718600 | tf_op jit(solution)/shard_map/ppermute | solution.py:45
  91.3 7.7 %collective-permute-start.21 = (bf16[256,768]{1,0:T(8,128)(2,1)S(1)}, bf16[256,768]{1,0:T(8,128)(2,1)S(1)}, u32[]{:S(2)}, u32[]{:S(2)}) collective-permute-start(bf16[256,768]{1,0:T(8,128)(2,1)S(1)} %broadcast_select_fusion.4), channel_id=1, source_target_pairs={{0,4},{4,0},{8,12},{12,8},{16,20},{20,16},{24,28},{28,24},{32,36},... | collective-permute-start | bytes 1179656 | tf_op jit(solution)/shard_map/ppermute | solution.py:45
  91.8 7.4 %collective-permute-start.22 = (bf16[256,768]{1,0:T(8,128)(2,1)S(1)}, bf16[256,768]{1,0:T(8,128)(2,1)S(1)}, u32[]{:S(2)}, u32[]{:S(2)}) collective-permute-start(bf16[256,768]{1,0:T(8,128)(2,1)S(1)} %broadcast_select_fusion.3), channel_id=1, source_target_pairs={{0,4},{4,0},{8,12},{12,8},{16,20},{20,16},{24,28},{28,24},{32,36},... | collective-permute-start | bytes 1179656 | tf_op jit(solution)/shard_map/ppermute | solution.py:45
  96.6 3.7 %collective-permute-start.28 = (bf16[256,768]{1,0:T(8,128)(2,1)S(1)}, bf16[256,768]{1,0:T(8,128)(2,1)S(1)}, u32[]{:S(2)}, u32[]{:S(2)}) collective-permute-start(bf16[256,768]{1,0:T(8,128)(2,1)S(1)} %broadcast_select_fusion.1), channel_id=1, source_target_pairs={{0,4},{4,0},{8,12},{12,8},{16,20},{20,16},{24,28},{28,24},{32,36},... | collective-permute-start | bytes 1179656 | tf_op jit(solution)/shard_map/ppermute | solution.py:45
  100.8 10.9 %collective-permute-start.29 = (bf16[4,64,768]{2,1,0:T(8,128)(2,1)S(1)}, bf16[4,64,768]{2,1,0:T(8,128)(2,1)S(1)}, u32[]{:S(2)}, u32[]{:S(2)}) collective-permute-start(bf16[4,64,768]{2,1,0:T(8,128)(2,1)S(1)} %get-tuple-element.37), channel_id=1, source_target_pairs={{0,64},{4,20},{8,72},{12,28},{16,80},{20,4},{24,88},{28,12},{32,96... | collective-permute-start | bytes 1179656 | tf_op jit(solution)/shard_map/ppermute | solution.py:108
  101.3 12.2 %collective-permute-start.30 = (bf16[4,64,768]{2,1,0:T(8,128)(2,1)S(1)}, bf16[4,64,768]{2,1,0:T(8,128)(2,1)S(1)}, u32[]{:S(2)}, u32[]{:S(2)}) collective-permute-start(bf16[4,64,768]{2,1,0:T(8,128)(2,1)S(1)} %get-tuple-element.36), channel_id=1, source_target_pairs={{0,32},{4,12},{8,40},{12,20},{16,48},{20,28},{24,56},{28,4},{32,64... | collective-permute-start | bytes 1179656 | tf_op jit(solution)/shard_map/ppermute | solution.py:108
  102.6 10.9 %collective-permute-start.31 = (bf16[4,64,768]{2,1,0:T(8,128)(2,1)S(1)}, bf16[4,64,768]{2,1,0:T(8,128)(2,1)S(1)}, u32[]{:S(2)}, u32[]{:S(2)}) collective-permute-start(bf16[4,64,768]{2,1,0:T(8,128)(2,1)S(1)} %get-tuple-element.35), channel_id=1, source_target_pairs={{0,96},{4,28},{8,104},{12,4},{16,112},{20,12},{24,120},{28,20},{32... | collective-permute-start | bytes 1179656 | tf_op jit(solution)/shard_map/ppermute | solution.py:108
  113.7 5.1 %collective-permute-start.33 = (bf16[64,768]{1,0:T(8,128)(2,1)S(1)}, bf16[64,768]{1,0:T(8,128)(2,1)S(1)}, u32[]{:S(2)}, u32[]{:S(2)}) collective-permute-start(bf16[64,768]{1,0:T(8,128)(2,1)S(1)} %get-tuple-element.42), channel_id=1, source_target_pairs={{0,16},{4,68},{8,24},{12,76},{16,0},{20,84},{24,8},{28,92},{32,48}... | collective-permute-start | bytes 294920 | tf_op jit(solution)/shard_map/ppermute | solution.py:108
  115.9 5.0 %collective-permute-start.34 = (bf16[64,768]{1,0:T(8,128)(2,1)S(1)}, bf16[64,768]{1,0:T(8,128)(2,1)S(1)}, u32[]{:S(2)}, u32[]{:S(2)}) collective-permute-start(bf16[64,768]{1,0:T(8,128)(2,1)S(1)} %get-tuple-element.41), channel_id=1, source_target_pairs={{0,8},{4,36},{8,16},{12,44},{16,24},{20,52},{24,0},{28,60},{32,40}... | collective-permute-start | bytes 294920 | tf_op jit(solution)/shard_map/ppermute | solution.py:108
  116.6 4.3 %collective-permute-start.35 = (bf16[64,768]{1,0:T(8,128)(2,1)S(1)}, bf16[64,768]{1,0:T(8,128)(2,1)S(1)}, u32[]{:S(2)}, u32[]{:S(2)}) collective-permute-start(bf16[64,768]{1,0:T(8,128)(2,1)S(1)} %get-tuple-element.40), channel_id=1, source_target_pairs={{0,24},{4,100},{8,0},{12,108},{16,8},{20,116},{24,16},{28,124},{32... | collective-permute-start | bytes 294920 | tf_op jit(solution)/shard_map/ppermute | solution.py:108
  121.0 8.6 %collective-permute-start.36 = (bf16[32,768]{1,0:T(8,128)(2,1)S(1)}, bf16[32,768]{1,0:T(8,128)(2,1)S(1)}, u32[]{:S(2)}, u32[]{:S(2)}) collective-permute-start(bf16[32,768]{1,0:T(8,128)(2,1)S(1)} %get-tuple-element.58), channel_id=1, source_target_pairs={{0,4},{4,0},{8,12},{12,8},{16,20},{20,16},{24,28},{28,24},{32,36},... | collective-permute-start | bytes 147464 | tf_op jit(solution)/shard_map/ppermute | solution.py:45
